TPU v7x, 256 devices: a whole 4x4x8 slice. The times are simulated.
256 devices in a mesh: row: 8 (over z_lo, core), col: 16 (over y, x), seq: 2 (over z_hi).
Axes of the slice: x: 4, y: 4, z: 8 (z_hi: 2, z_lo: 4; z = z_hi * 4 + z_lo), core: 2. Of those that a mesh axis runs over, the one named last changes fastest.
Arguments:
- alignment: bfloat16 [64, 1024, 256], P('seq', ('row', 'col')), may hold values from -6 to 6
- left_weight: bfloat16 [256, 32], replicated, may hold values from -0.375 to 0.375
- right_weight: bfloat16 [256, 32], replicated, may hold values from -0.375 to 0.375
- out_weight: bfloat16 [1024, 128], replicated, may hold values from -0.1875 to 0.1875
- out_bias: float32 [128], replicated, may hold values from -3 to 3
- cotangent: bfloat16 [1024, 1024, 128], P(('row', 'seq'), 'col'), may hold values from -6 to 6
Outputs:
- pair_update: bfloat16 [1024, 1024, 128], P(('row', 'seq'), 'col')
- alignment_grad: float32 [64, 1024, 256], P('seq', ('row', 'col'))
- left_weight_grad: float32 [256, 32], replicated
- right_weight_grad: float32 [256, 32], replicated
- out_weight_grad: float32 [1024, 128], replicated
All inputs are finite; a program needn't handle non-finite values.
Results may differ from a plain program's by a relative error of at most 0.02.
Values may be sent and summed in bfloat16 or wider, within the bound.
No kernel may reach another device: no remote copies, remote signals or barrier semaphores. Data moves between devices by JAX's collectives and lax.ppermute only.
A program may use at most 64 MiB of HBM per device.

v0:
```python
import math

import jax
import jax.numpy as jnp
from jax import lax
from jax.sharding import PartitionSpec as P


def body(alignment, left_weight, right_weight, out_weight, out_bias, cotangent):
    proj_width = left_weight.shape[1]
    pair_width = out_weight.shape[1]
    values = alignment.astype(jnp.float32)
    center = values - jnp.mean(values, axis=2, keepdims=True)
    invstd = lax.rsqrt(jnp.mean(center * center, axis=2, keepdims=True) + 1e-05)
    scaled = center * invstd
    normed = scaled.astype(jnp.bfloat16)
    both_weights = jnp.concatenate([left_weight, right_weight], axis=1)
    projected = jnp.einsum(
        "srk,kc->src", normed, both_weights, preferred_element_type=jnp.float32
    ).astype(jnp.bfloat16)
    slab = lax.all_gather(projected, "col", axis=1, tiled=True)
    left_rows = lax.all_to_all(
        slab[:, :, :proj_width], "seq", split_axis=1, concat_axis=0, tiled=True
    )
    ratio = lax.axis_size("col") // lax.axis_size("row")
    col_index = lax.axis_index("col")
    slab_len = slab.shape[1]
    col_width = slab_len // ratio
    every_col = lax.all_gather(projected[:, :, proj_width:], ("row", "col"), axis=1, tiled=True)
    own_cols = lax.dynamic_slice_in_dim(every_col, col_index * col_width, col_width, 1)
    right_cols = lax.all_gather(own_cols, "seq", axis=0, tiled=True)
    seq_total = right_cols.shape[0]
    inverse = 1.0 / seq_total
    row_count = left_rows.shape[1]
    block_rows = math.gcd(8, row_count)
    block_count = row_count // block_rows
    left_blocks = left_rows.reshape(seq_total, block_count, block_rows, proj_width).transpose(
        1, 0, 2, 3
    )
    cot_blocks = cotangent.reshape(block_count, block_rows * col_width, pair_width)

    def one_block(carry, inputs):
        wout_total, right_total = carry
        left_piece, cot_flat = inputs
        outer = (
            jnp.einsum("sic,sjd->ijcd", left_piece, right_cols, preferred_element_type=jnp.float32)
            * inverse
        )
        outer_flat = outer.astype(jnp.bfloat16).reshape(
            block_rows * col_width, proj_width * proj_width
        )
        pair = (
            jnp.dot(outer_flat, out_weight, preferred_element_type=jnp.float32) + out_bias
        ).astype(jnp.bfloat16)
        wout_total = wout_total + lax.dot_general(
            outer_flat, cot_flat, (((0,), (0,)), ((), ())), preferred_element_type=jnp.float32
        )
        outer_grad = (
            jnp.dot(cot_flat, out_weight.T, preferred_element_type=jnp.float32) * inverse
        ).astype(jnp.bfloat16)
        outer_grad = outer_grad.reshape(block_rows, col_width, proj_width, proj_width)
        left_part = jnp.einsum(
            "ijcd,sjd->sic", outer_grad, right_cols, preferred_element_type=jnp.float32
        )
        right_total = right_total + jnp.einsum(
            "ijcd,sic->sjd", outer_grad, left_piece, preferred_element_type=jnp.float32
        )
        return (
            (wout_total, right_total),
            (pair.reshape(block_rows, col_width, pair_width), left_part),
        )

    init = (
        jnp.zeros((proj_width * proj_width, pair_width), jnp.float32),
        jnp.zeros((seq_total, col_width, proj_width), jnp.float32),
    )
    (wout_part, right_part), (pairs, left_parts) = lax.scan(
        one_block, init, (left_blocks, cot_blocks)
    )
    pair_update = pairs.reshape(row_count, col_width, pair_width)
    left_grad = left_parts.transpose(1, 0, 2, 3).reshape(seq_total, row_count, proj_width)
    left_back = lax.all_to_all(
        left_grad.astype(jnp.bfloat16), "seq", split_axis=0, concat_axis=1, tiled=True
    ).astype(left_grad.dtype)
    right_seq = lax.psum_scatter(
        right_part.astype(jnp.bfloat16), "seq", scatter_dimension=0, tiled=True
    ).astype(jnp.float32)
    left_local = lax.psum_scatter(
        left_back.astype(jnp.bfloat16), "col", scatter_dimension=1, tiled=True
    ).astype(jnp.float32)
    spread = jnp.zeros(
        (right_seq.shape[0], slab_len * lax.axis_size("row"), proj_width), jnp.float32
    )
    spread = lax.dynamic_update_slice_in_dim(spread, right_seq, col_index * col_width, 1)
    right_local = lax.psum_scatter(spread, ("row", "col"), scatter_dimension=1, tiled=True)
    grads_both = jnp.concatenate([left_local, right_local], axis=2).astype(jnp.bfloat16)
    weight_part = jnp.einsum("srk,src->kc", normed, grads_both, preferred_element_type=jnp.float32)
    normed_grad = jnp.einsum(
        "src,kc->srk", grads_both, both_weights, preferred_element_type=jnp.float32
    )
    mean_grad = jnp.mean(normed_grad, axis=2, keepdims=True)
    mean_cross = jnp.mean(normed_grad * scaled, axis=2, keepdims=True)
    alignment_grad = invstd * (normed_grad - mean_grad - scaled * mean_cross)
    weight_total, wout_total = lax.psum((weight_part, wout_part), ("row", "col", "seq"))
    residue_total = alignment.shape[1] * lax.axis_size("row") * lax.axis_size("col")
    left_weight_grad = weight_total[:, :proj_width] / residue_total
    right_weight_grad = weight_total[:, proj_width:] / residue_total
    return (
        pair_update,
        alignment_grad,
        left_weight_grad,
        right_weight_grad,
        wout_total / residue_total,
    )


def solution(mesh):
    placed = (P("seq", ("row", "col"), None), P(), P(), P(), P(), P(("row", "seq"), "col", None))
    return jax.shard_map(
        body,
        mesh=mesh,
        in_specs=placed,
        out_specs=(P(("row", "seq"), "col", None), P("seq", ("row", "col"), None), P(), P(), P()),
        check_vma=False,
    )
```

profile of v0, /device:TPU:1, one launch (start us, length us, event | category | flops | bytes accessed | tf_op | source)
XLA Modules:
  0.0 1552.9 jit_solution(436616771850505572)
XLA Ops:
  11.2 23.8 %all_gather.9 = bf16[32,128,64]{2,1,0:T(8,128)(2,1)S(1)} all-gather(bf16[32,8,64]{2,1,0:T(8,128)(2,1)S(1)} %convolution_convert_fusion), channel_id=1, replica_groups=mesh['row'=8,'col'=16,'seq'=2] {'col'}, dimensions={1}, use_global_device_ids=true | all-gather | bytes 557056 | tf_op jit(solution)/shard_map/all_gather | solution.py:21
  35.8 1.7 reshape.65
  37.5 7.2 all-to-all-start
  44.7 8.2 all-to-all-done
  55.6 240.9 %all-gather.2.cloned.1.call-done = bf16[32,1024,32]{2,1,0:T(8,128)(2,1)} async-done(((bf16[32,8,32]{2,1,0:T(8,128)(2,1)}), bf16[32,1024,32]{2,1,0:T(8,128)(2,1)}) %all-gather.2.cloned.1.call-update) | async-done | bytes 2097168 | tf_op jit(solution)/shard_map/all_gather | solution.py:29
  297.8 15.0 all_gather.11
  313.9 137.8 %while.17 = (s32[]{:T(128)}, f32[1024,128]{1,0:T(8,128)}, f32[64,64,32]{1,0,2:T(8,128)}, bf16[8,8,64,128]{3,2,1,0:T(8,128)(2,1)}, bf16[8,64,8,32]{1,3,2,0:T(8,12...) while((s32[]{:T(128)}, f32[1024,128]{1,0:T(8,128)}, ...), condition=%wide.region_3.4_spmd.clone, body=%wide.region_2.3_spmd.clone.sunk | while | flops 606732288 | bytes 24249076 | solution.py:77
  316.9 3.2 fusion.83
  320.0 2.3 fusion.81
  323.4 1.5 fusion.80
  328.1 2.1 convolution_add_fusion.3
  333.9 3.2 fusion.83
  337.1 2.3 fusion.81
  340.5 1.5 fusion.80
  345.1 2.4 convolution_add_fusion.3
  351.2 3.2 fusion.83
  354.3 2.3 fusion.81
  357.7 1.5 fusion.80
  362.4 2.3 convolution_add_fusion.3
  368.4 3.2 fusion.83
  371.6 2.3 fusion.81
  375.0 1.5 fusion.80
  379.6 2.4 convolution_add_fusion.3
  385.7 3.2 fusion.83
  388.8 2.3 fusion.81
  392.2 1.5 fusion.80
  396.9 2.3 convolution_add_fusion.3
  402.9 3.2 fusion.83
  406.1 2.3 fusion.81
  409.5 1.5 fusion.80
  414.1 2.3 convolution_add_fusion.3
  420.2 3.2 fusion.83
  423.3 2.3 fusion.81
  426.7 1.5 fusion.80
  431.4 2.3 convolution_add_fusion.3
  437.4 3.2 fusion.83
  440.6 2.3 fusion.81
  444.0 1.5 fusion.80
  448.6 2.3 convolution_add_fusion.3
  451.6 2.7 copy.107
  456.1 11.1 all_to_all.33
  469.0 14.1 reduce-scatter.4.cloned.1.call-done
  484.3 7.7 broadcast_in_dim.32
  494.9 85.6 %all-reduce.5.cloned.1.call-done = bf16[32,128,32]{2,1,0:T(8,128)(2,1)} async-done(((bf16[32,128,32]{2,1,0:T(8,128)(2,1)}), bf16[32,128,32]{2,1,0:T(8,128)(2,1)}) %all-reduce.5.cloned.1.call-update) | async-done | bytes 262160
  581.3 673.8 %reduce-scatter.6.cloned.1.call-done = f32[32,8,32]{2,1,0:T(8,128)} async-done(((f32[32,1024,32]{2,1,0:T(8,128)}), f32[32,8,32]{2,1,0:T(8,128)}) %reduce-scatter.6.cloned.1.call-update) | async-done | bytes 32784 | tf_op jit(solution)/shard_map/reduce_scatter | solution.py:95
  1258.3 284.8 %all-reduce.7.cloned.1.call-done = (f32[256,64]{0,1:T(8,128)}, f32[1024,128]{1,0:T(8,128)}) async-done(((f32[256,64]{0,1:T(8,128)}, f32[1024,128]{1,0:T(8,128)}), (f32[256,64]{0,1:T(8,128)}, f32[1024,128]{1,0:T(8,128)})) %all-reduce.7.cloned.1.call-update) | async-done | bytes 589840 | tf_op jit(solution)/shard_map/psum | solution.py:104
  1543.1 1.4 slice_multiply_fusion
  1544.5 1.9 broadcast_multiply_fusion
  (158 shorter events, 82.9 us)
Async XLA Ops:
  7.2 289.3 %all-gather.2.cloned.1.call-start = ((), (), s32[]{:S(2)}) async-start(), calls=%async_computation.4 | async-start | bytes 8454144 | tf_op jit(solution)/shard_map/all_gather | solution.py:29
  37.5 15.4 all-to-all-start
  44.7 438.4 %reduce-scatter.4.cloned.1.call-start = ((), (), s32[]{:S(2)}) async-start(), calls=%async_computation.5 | async-start | bytes 786432 | tf_op jit(solution)/shard_map/reduce_scatter | solution.py:85
  55.6 258.2 %copy-start.2 = (bf16[1024,128]{1,0:T(8,128)(2,1)S(1)}, bf16[1024,128]{1,0:T(8,128)(2,1)}, u32[]{:S(2)}) copy-start(bf16[1024,128]{1,0:T(8,128)(2,1)} %param.11) | copy-start | bytes 786436
  55.6 258.2 %copy-start.6 = (f32[128]{0:T(128)S(1)}, f32[128]{0:T(128)}, u32[]{:S(2)}) copy-start(f32[128]{0:T(128)} %param.12) | copy-start | bytes 1540
  316.9 3.2 copy-start
  320.0 3.4 copy-start.3
  322.4 1.1 copy-start.1
  333.9 3.2 copy-start
  337.1 3.4 copy-start.3
  339.4 1.1 copy-start.1
  351.1 3.2 copy-start
  354.3 3.4 copy-start.3
  356.7 1.1 copy-start.1
  368.4 3.2 copy-start
  371.6 3.4 copy-start.3
  373.9 1.1 copy-start.1
  385.7 3.2 copy-start
  388.8 3.4 copy-start.3
  391.2 1.1 copy-start.1
  402.9 3.2 copy-start
  406.1 3.4 copy-start.3
  408.4 1.1 copy-start.1
  420.1 3.2 copy-start
  423.3 3.4 copy-start.3
  425.7 1.1 copy-start.1
  437.4 3.2 copy-start
  440.6 3.4 copy-start.3
  442.9 1.1 copy-start.1
  451.6 3.0 copy-start.5
  454.3 126.1 %all-reduce.5.cloned.1.call-start = ((), (), s32[]{:S(2)}) async-start(), calls=%async_computation.7 | async-start | bytes 2097152
  468.9 786.2 %reduce-scatter.6.cloned.1.call-start = ((), (), s32[]{:S(2)}) async-start(), calls=%async_computation.6 | async-start | bytes 16908288 | tf_op jit(solution)/shard_map/reduce_scatter | solution.py:95
  493.0 0.7 copy-start.9
  493.0 763.1 %copy-start.4 = (bf16[32,8,256]{2,1,0:T(8,128)(2,1)S(1)}, bf16[32,8,256]{2,1,0:T(8,128)(2,1)}, u32[]{:S(2)}) copy-start(bf16[32,8,256]{2,1,0:T(8,128)(2,1)} %param.8) | copy-start | bytes 393220
  493.0 764.0 %copy-start.7 = (bf16[256,32]{0,1:T(8,128)(2,1)S(1)}, bf16[256,32]{0,1:T(8,128)(2,1)}, u32[]{:S(2)}) copy-start(bf16[256,32]{0,1:T(8,128)(2,1)} %param.10) | copy-start | bytes 49156
  493.0 764.0 %copy-start.8 = (bf16[256,32]{0,1:T(8,128)(2,1)S(1)}, bf16[256,32]{0,1:T(8,128)(2,1)}, u32[]{:S(2)}) copy-start(bf16[256,32]{0,1:T(8,128)(2,1)} %param.9) | copy-start | bytes 49156
  493.0 1050.1 %all-reduce.7.cloned.1.call-start = ((), (), s32[]{:S(2)}) async-start(), calls=%async_computation.8 | async-start | bytes 1179648 | tf_op jit(solution)/shard_map/psum | solution.py:104
Sparse Core Ops, SparseCore 0:
  11.4 285.0 all-gather.1
  454.5 28.5 reduce-scatter.3
  486.7 93.7 all-reduce.4
  583.0 672.0 reduce-scatter.5
  1262.2 280.8 all-reduce.6
where the time goes:
time: 1550 us
  waiting for transfers between devices  1310 us (85%)
  matrix products  91.7 us (6%)
  local copies, waits for them, and re-layouts  73.7 us (5%)
  blocking collectives  49.9 us (3%)
    reduce_scatter x1, waiting for transfers between devices, body(): lax.psum_scatter(spread, ('row', 'col'), scatter_dimension=1, tiled=True)  674 us
    psum x1, waiting for transfers between devices, body(): lax.psum((weight_part, wout_part), ('row', 'col', 'seq'))  285 us
    all_gather x1, waiting for transfers between devices, body(): lax.all_gather(projected[:, :, proj_width:], ('row', 'col'), axis=1, tile...  241 us
    unnamed x6, waiting for transfers between devices  85.7 us
  transfers between devices with their start and end apart: 6, of which 6 were waited for; matrix products, arithmetic and copies ran while one was open for 1% of the time, Pallas kernels for 0%

commit v1 on v0

v1 whole, which is shorter than its diff:
```python
import jax
import jax.numpy as jnp
from jax import lax
from jax.experimental import pallas as pl
from jax.experimental.pallas import tpu as pltpu
from jax.sharding import PartitionSpec as P

F32 = jnp.float32
BF16 = jnp.bfloat16
LANES = 128
CP = 32
SEQ_HALF = 32
EPS = 1e-05


def dot(a, b, dims):
    return lax.dot_general(a, b, ((dims[:1], dims[1:]), ((), ())), preferred_element_type=F32)


def params(mib):
    return pltpu.CompilerParams(vmem_limit_bytes=mib << 20)


def normalize(x_ref, rows_ref):
    rows = x_ref[...].astype(F32).reshape(256, 256)
    halves = []
    for h in range(2):
        rows_ref[h] = rows[:, h * 128 : h * 128 + 128]
        halves.append(
            jnp.concatenate([rows_ref[h, pl.ds(i, SEQ_HALF, stride=8), :] for i in range(8)], axis=0)
        )
    values = jnp.concatenate(halves, axis=1)
    center = values - jnp.mean(values, axis=1, keepdims=True)
    invstd = lax.rsqrt(jnp.mean(center * center, axis=1, keepdims=True) + EPS)
    return center * invstd, invstd


def project_kernel(x_ref, weights_ref, left_ref, right_ref, rows_ref, block_ref):
    scaled, _ = normalize(x_ref, rows_ref)
    both = dot(weights_ref[...], scaled.astype(BF16), (1, 1))
    left_ref[0:32, :] = both[0:32, 0:128].astype(BF16)
    left_ref[32:64, :] = both[0:32, 128:256].astype(BF16)
    for j in range(8):
        block_ref[j * 8 : j * 8 + 8, :] = jnp.concatenate(
            [both[32 + k * 8 : 40 + k * 8, j * 32 : j * 32 + 32] for k in range(4)], axis=1
        )
    right_ref[...] = jnp.concatenate(
        [block_ref[pl.ds(h, 8, stride=8), :] for h in range(8)], axis=0
    ).astype(BF16)


def pair_kernel(
    left_in, right_in, cot_ref, w_scaled_ref, w_turned_ref, bias_ref,
    pair_ref, left_out, right_out, wout_ref,
    gathered, spread, left_ref, left_t_ref, grad, outer, left_sum, right_sum, wout_sum, wout_rows,
):
    lane = lax.broadcasted_iota(jnp.int32, (64, LANES), 1)
    for b in range(8):
        for half in range(2):
            left_ref[b * 64 : b * 64 + 64, half * 128 : half * 128 + 128] = left_in[b * 2 + half]
    left_t_ref[...] = left_ref[...].astype(F32).T.astype(BF16)
    gathered[...] = right_in[...].astype(F32)
    for h in range(8):
        for half in range(2):
            tile = jnp.concatenate(
                [gathered[r * 2 + half, h * 8 : h * 8 + 8, :] for r in range(8)], axis=0
            )
            turned = [tile] + [pltpu.roll(tile, k * 32, 1) for k in range(1, 4)]
            for d in range(4):
                for i in range(4):
                    spread[
                        h, d * 256 + i * 64 : d * 256 + i * 64 + 64, half * 128 : half * 128 + 128
                    ] = jnp.where(lane // 32 == i, turned[(i - d) % 4], 0.0).astype(BF16)

    def outer_grad_step(i, carry):
        cot = cot_ref[pl.ds(i * 4, 4)].reshape(256, LANES)
        rows = pl.ds(pl.multiple_of(i * 32, 32), 32)
        for h in range(8):
            piece = dot(w_scaled_ref[h * 128 : h * 128 + 128, :], cot, (1, 1)).astype(BF16)
            for d in range(4):
                grad[h, rows, d * 256 : d * 256 + 256] = piece[d * 32 : d * 32 + 32]
        return carry

    lax.fori_loop(0, 16, outer_grad_step, 0)

    left_sum[...] = jnp.zeros_like(left_sum)
    low = lax.broadcasted_iota(jnp.int32, (32, LANES), 1) < 64

    def grads_step(h, carry):
        left_sum[...] += dot(grad[h], spread[h], (1, 0))
        for half in range(2):
            parts = []
            part = dot(left_t_ref[half * 128 : half * 128 + 128, :], grad[h], (1, 0))
            for d in range(4):
                lo = part[:, d * 256 : d * 256 + 128]
                hi = part[:, d * 256 + 128 : d * 256 + 256]
                parts.append(
                    jnp.where(low, lo[0:32], lo[32:64]) + jnp.where(low, hi[64:96], hi[96:128])
                )
            turned = jnp.concatenate(parts, axis=0).T
            total = turned[0:64] + turned[64:128]
            for r in range(8):
                right_sum[r * 2 + half, pl.ds(pl.multiple_of(h * 8, 8), 8), :] = total[
                    r * 8 : r * 8 + 8
                ]
        return carry

    lax.fori_loop(0, 8, grads_step, 0)
    right_out[...] = right_sum[...].astype(BF16)
    for b in range(8):
        for half in range(2):
            left_out[b * 2 + half] = left_sum[
                b * 64 : b * 64 + 64, half * 128 : half * 128 + 128
            ].astype(BF16)

    left_ref[...] = (left_ref[...].astype(F32) * (1.0 / 64.0)).astype(BF16)

    def outer_step(h, carry):
        for d in range(4):
            piece = dot(left_ref[...], spread[h, d * 256 : d * 256 + 256, :], (1, 1)).astype(BF16)
            outer[:, pl.ds(pl.multiple_of(h * 128 + d * 32, 32), 32), :] = piece.reshape(16, 32, 256)
        return carry

    lax.fori_loop(0, 8, outer_step, 0)
    wout_sum[...] = jnp.zeros_like(wout_sum)

    def pair_step(i, carry):
        cot = cot_ref[pl.ds(i * 4, 4)].reshape(256, LANES)
        tile = outer[i]
        turned = dot(w_turned_ref[...], tile, (1, 0))
        pair_ref[pl.ds(i * 4, 4)] = (
            (turned.T + bias_ref[...]).astype(BF16).reshape(4, 64, LANES)
        )
        wout_sum[...] += dot(tile, cot, (1, 0))
        return carry

    lax.fori_loop(0, 16, pair_step, 0)
    for d in range(32):
        wout_rows[pl.ds(d, 32, stride=32), :] = wout_sum[d * 32 : d * 32 + 32, :]
    wout_ref[...] = wout_rows[...].astype(BF16)


def finish_kernel(x_ref, weights_ref, left_ref, right_ref, align_ref, weight_ref, rows_ref, block_ref):
    scaled, invstd = normalize(x_ref, rows_ref)
    block_ref[...] = right_ref[...].astype(F32)
    rows = [block_ref[pl.ds(j, 8, stride=8), :] for j in range(8)]
    right = jnp.concatenate(
        [
            jnp.concatenate([rows[j][:, k * 32 : k * 32 + 32] for j in range(8)], axis=1)
            for k in range(4)
        ],
        axis=0,
    )
    left = jnp.concatenate([left_ref[0:32, :], left_ref[32:64, :]], axis=1).astype(F32)
    grads = jnp.concatenate([left, right], axis=0).astype(BF16)
    weight = dot(grads, scaled.astype(BF16), (1, 0))
    weight_ref[0:64, :] = weight[:, 0:128].astype(BF16)
    weight_ref[64:128, :] = weight[:, 128:256].astype(BF16)
    normed_grad = dot(grads, weights_ref[...], (0, 0))
    mean_grad = jnp.mean(normed_grad, axis=1, keepdims=True)
    mean_cross = jnp.mean(normed_grad * scaled, axis=1, keepdims=True)
    result = invstd * (normed_grad - mean_grad - scaled * mean_cross)
    for h in range(2):
        for i in range(8):
            rows_ref[h, pl.ds(i, SEQ_HALF, stride=8), :] = result[
                i * 32 : i * 32 + 32, h * 128 : h * 128 + 128
            ]
        align_ref[:, h * 128 : h * 128 + 128] = rows_ref[h]


def body(alignment, left_weight, right_weight, out_weight, out_bias, cotangent):
    rows_n, cols_n, seq_n = lax.axis_size("row"), lax.axis_size("col"), lax.axis_size("seq")
    tile = ("row", "seq")
    to_left = [
        (c * seq_n + s, ((c % 8) * 2 + s) * seq_n + c // 8) for c in range(cols_n) for s in range(seq_n)
    ]
    to_right = [
        (r * cols_n + c, (c % 8) * cols_n + 2 * r + c // 8) for r in range(rows_n) for c in range(cols_n)
    ]
    swap = lambda pairs: [(b, a) for a, b in pairs]

    weights = jnp.concatenate(
        [left_weight.T, right_weight.T.reshape(8, 4, 256).transpose(1, 0, 2).reshape(32, 256)], axis=0
    )
    w_rows = out_weight.reshape(CP, CP, LANES).transpose(1, 0, 2).reshape(CP * CP, LANES)
    w_scaled = (w_rows.astype(F32) * (1.0 / 64.0)).astype(BF16)
    w_turned = w_rows.T

    block = jax.ShapeDtypeStruct((64, LANES), BF16)
    left_block, right_block = pl.pallas_call(
        project_kernel,
        out_shape=(block, block),
        scratch_shapes=[pltpu.VMEM((2, 256, LANES), F32), pltpu.VMEM((64, LANES), F32)],
        compiler_params=params(16),
        name="project",
    )(alignment, weights)

    left_block = lax.ppermute(left_block, ("col", "seq"), to_left)
    right_block = lax.ppermute(right_block, ("row", "col"), to_right)

    def gather(value, axes):
        return lax.all_to_all(
            jnp.broadcast_to(value, (16,) + value.shape), axes, 0, 0, tiled=True
        )

    left_all = gather(left_block, "col")
    right_all = gather(right_block, tile)

    blocks = jax.ShapeDtypeStruct((16, 64, LANES), BF16)
    pair, left_part, right_part, wout_part = pl.pallas_call(
        pair_kernel,
        out_shape=(
            jax.ShapeDtypeStruct((64, 64, LANES), BF16),
            blocks,
            blocks,
            jax.ShapeDtypeStruct((1024, LANES), BF16),
        ),
        scratch_shapes=[
            pltpu.VMEM((16, 64, LANES), F32),
            pltpu.VMEM((8, 1024, 256), BF16),
            pltpu.VMEM((512, 256), BF16),
            pltpu.VMEM((256, 512), BF16),
            pltpu.VMEM((8, 512, 1024), BF16),
            pltpu.VMEM((16, 1024, 256), BF16),
            pltpu.VMEM((512, 256), F32),
            pltpu.VMEM((16, 64, LANES), F32),
            pltpu.VMEM((1024, LANES), F32),
            pltpu.VMEM((1024, LANES), F32),
        ],
        compiler_params=params(48),
        name="pair_tile",
    )(left_all, right_all, cotangent, w_scaled, w_turned, out_bias.reshape(1, LANES))

    def total(value):
        return jnp.sum(value.astype(F32), axis=0)

    first = lax.all_to_all(
        jnp.concatenate([right_part, wout_part.reshape(16, 64, LANES)], axis=1), tile, 0, 0, tiled=True
    )
    first = total(first).astype(BF16)
    second = lax.all_to_all(
        jnp.concatenate([left_part, first[64:].reshape(16, 4, LANES)], axis=1), "col", 0, 0, tiled=True
    )
    second = total(second).astype(BF16)
    wout_piece = second[64:]
    left_grad = lax.ppermute(second[:64], ("col", "seq"), swap(to_left))
    right_grad = lax.ppermute(first[:64], ("row", "col"), swap(to_right))

    align_grad, weight_part = pl.pallas_call(
        finish_kernel,
        out_shape=(
            jax.ShapeDtypeStruct((256, 256), F32),
            jax.ShapeDtypeStruct((128, LANES), BF16),
        ),
        scratch_shapes=[pltpu.VMEM((2, 256, LANES), F32), pltpu.VMEM((64, LANES), F32)],
        compiler_params=params(16),
        name="finish",
    )(alignment, weights, left_grad, right_grad)

    weight_piece = total(
        lax.all_to_all(weight_part.reshape(16, 8, LANES), tile, 0, 0, tiled=True)
    ).astype(BF16)
    third = gather(jnp.concatenate([weight_piece, wout_piece], axis=0), "col")
    weight_piece = total(third[:, :8]).astype(BF16)
    last = gather(
        jnp.concatenate([third[:, 8:].reshape(64, LANES), weight_piece], axis=0), tile
    ).astype(F32) * (1.0 / 1024.0)
    wout_grad = last[:, :64].reshape(1024, LANES)
    halves = last[:, 64:].reshape(2, 64, LANES)
    weight_grad = jnp.concatenate([halves[0], halves[1]], axis=1)
    left_weight_grad = weight_grad[:32].T
    right_weight_grad = weight_grad[32:].reshape(4, 8, 256).transpose(1, 0, 2).reshape(32, 256).T
    return (
        pair,
        align_grad.reshape(alignment.shape),
        left_weight_grad,
        right_weight_grad,
        wout_grad,
    )


def solution(mesh):
    placed = (P("seq", ("row", "col"), None), P(), P(), P(), P(), P(("row", "seq"), "col", None))
    return jax.shard_map(
        body,
        mesh=mesh,
        in_specs=placed,
        out_specs=(P(("row", "seq"), "col", None), P("seq", ("row", "col"), None), P(), P(), P()),
        check_vma=False,
    )
```

time: 1550 us -> 170 us (0.11)
  waiting for transfers between devices: 1310 us -> 21.7 us
  matrix products: 91.7 us -> 0 us
  local copies, waits for them, and re-layouts: 73.7 us -> 4.77 us
  starting transfers between devices: 7.54 us -> 66.7 us
  Pallas kernels: 0 us -> 24.7 us
    reduce_scatter x2 -> x0, waiting for transfers between devices: 688 us -> none  [the longest x1 674 us: body(): lax.psum_scatter(spread, ('row', 'col'), scatter_dimension=1, tiled=True)]
    psum x1 -> x0, waiting for transfers between devices: 285 us -> none  [body(): lax.psum((weight_part, wout_part), ('row', 'col', 'seq'))]
    all_gather x1 -> x0, waiting for transfers between devices: 241 us -> none  [body(): lax.all_gather(projected[:, :, proj_width:], ('row', 'col'), axis=1, tile...]
    dot_general x51 -> x0, matrix products: 91.7 us -> none  [the longest x8 25.4 us: one_block(): jnp.einsum('ijcd,sjd->sic', outer_grad, right_cols, preferred_element_typ...]
    unnamed x6 -> x0, waiting for transfers between devices: 85.7 us -> none
    all_to_all x1 -> x4, starting transfers between devices: 7.19 us -> 53 us  [the longest x2 29.4 us: gather(): lax.all_to_all(jnp.broadcast_to(value, (16,) + value.shape), axes, 0, 0,...]
    all_gather x2 -> x0, blocking collectives: 38.9 us -> none  [the longest x1 23.8 us: body(): slab = lax.all_gather(projected, 'col', axis=1, tiled=True)]
    all_to_all x1 -> x3, blocking collectives: 11.1 us -> 48.5 us  [the longest x2 28.7 us: gather(): lax.all_to_all(jnp.broadcast_to(value, (16,) + value.shape), axes, 0, 0,...]
  transfers between devices with their start and end apart: 6 -> 8, of which waited for: 6 -> 4; matrix products, arithmetic and copies ran while one was open for 1% -> 0% of each run, Pallas kernels for 0% -> 0%
where the time goes in v1:
time: 170 us
  starting transfers between devices  66.7 us (39%)
  blocking collectives  48.5 us (29%)
  Pallas kernels  24.7 us (15%)
  waiting for transfers between devices  21.7 us (13%)
  local copies, waits for them, and re-layouts  4.77 us (3%)
  other arithmetic  2.41 us (1%)
    all_to_all x2, starting transfers between devices, gather(): lax.all_to_all(jnp.broadcast_to(value, (16,) + value.shape), axes, 0, 0,...  29.4 us
    all_to_all x2, blocking collectives, gather(): lax.all_to_all(jnp.broadcast_to(value, (16,) + value.shape), axes, 0, 0,...  28.7 us
    pallas_call x1, Pallas kernels, body(): pl.pallas_call(pair_kernel, out_shape=(jax.ShapeDtypeStruct((64, 64, LANE...  23 us
    all_to_all x1, blocking collectives, body(): lax.all_to_all(jnp.concatenate([right_part, wout_part.reshape(16, 64, LAN...  19.8 us
    all_to_all x1, starting transfers between devices, body(): lax.all_to_all(weight_part.reshape(16, 8, LANES), tile, 0, 0, tiled=True)  15.1 us
    all_to_all x2, waiting for transfers between devices, gather(): lax.all_to_all(jnp.broadcast_to(value, (16,) + value.shape), axes, 0, 0,...  11 us
    all_to_all x1, starting transfers between devices, body(): lax.all_to_all(jnp.concatenate([left_part, first[64:].reshape(16, 4, LANE...  8.54 us
    all_to_all x1, waiting for transfers between devices, body(): lax.all_to_all(weight_part.reshape(16, 8, LANES), tile, 0, 0, tiled=True)  7.29 us
  transfers between devices with their start and end apart: 8, of which 4 were waited for; matrix products, arithmetic and copies ran while one was open for 0% of the time, Pallas kernels for 0%

profile of v1, /device:TPU:1, one launch (start us, length us, event | category | flops | bytes accessed | tf_op | source)
XLA Modules:
  0.0 169.6 jit_solution(17045543050011683736)
XLA Ops:
  0.6 0.0 copy-start.1
  0.6 0.8 reshape.54
  1.4 0.7 pad_maximum_fusion.3.weights_ref
  2.1 0.0 copy-done.1
  2.1 0.5 project.1
  2.6 0.7 collective-permute-start
  3.3 0.0 collective-permute-done
  3.3 0.8 broadcast_in_dim.12
  4.1 18.3 %all-to-all-start = ((bf16[16,64,128]{2,1,0:T(8,128)(2,1)}), bf16[16,64,128]{2,1,0:T(8,128)(2,1)S(1)}, u32[]{:S(2)}, u32[]{:S(2)}) async-start(bf16[16,64,128]{2,1,0:T(8,128)(2,1)} %broadcast_in_dim.12), calls=%async_computation | async-start | bytes 524288 | tf_op jit(solution)/shard_map/all_to_all | solution.py:202
  22.4 7.0 %collective-permute-start.1 = (bf16[64,128]{1,0:T(8,128)(2,1)S(1)}, bf16[64,128]{1,0:T(8,128)(2,1)S(1)}, u32[]{:S(2)}, u32[]{:S(2)}) collective-permute-start(bf16[64,128]{1,0:T(8,128)(2,1)S(1)} %get-tuple-element.14), channel_id=1, source_target_pairs={{0,0},{2,32},{4,64},{6,96},{8,128},{10,160},{12,192},{14,224},{16,... | collective-permute-start | bytes 49160 | tf_op jit(solution)/shard_map/ppermute | solution.py:199
  29.5 0.8 collective-permute-done.1
  30.3 0.0 all-to-all-done.left_in
  30.3 0.0 copy-start.3
  30.3 0.8 broadcast_in_dim.13
  31.1 0.0 copy-start
  31.1 11.0 %all-to-all-start.1 = ((bf16[16,64,128]{2,1,0:T(8,128)(2,1)}), bf16[16,64,128]{2,1,0:T(8,128)(2,1)S(1)}, u32[]{:S(2)}, u32[]{:S(2)}) async-start(bf16[16,64,128]{2,1,0:T(8,128)(2,1)} %broadcast_in_dim.13), calls=%async_computation.1 | async-start | bytes 524288 | tf_op jit(solution)/shard_map/all_to_all | solution.py:202
  42.1 0.0 copy-done.3
  42.1 0.1 copy.19
  42.2 0.1 copy.20
  42.4 0.1 multiply_convert_fusion.w_scaled_ref
  42.5 11.0 %all-to-all-done.1.right_in = bf16[16,64,128]{2,1,0:T(8,128)(2,1)S(1)} async-done(((bf16[16,64,128]{2,1,0:T(8,128)(2,1)}), bf16[16,64,128]{2,1,0:T(8,128)(2,1)S(1)}, u32[]{:S(2)}, u32[]{:S(2)}) %all-to-all-start.1) | async-done | bytes 262176 | tf_op jit(solution)/shard_map/all_to_all | solution.py:202
  53.5 0.0 copy-start.2
  53.5 0.0 copy-done
  53.5 0.7 copy-done.2
  54.1 23.0 %pair_tile.1 = (bf16[64,64,128]{2,1,0:T(8,128)(2,1)}, bf16[16,64,128]{2,1,0:T(8,128)(2,1)S(1)}, bf16[16,64,128]{2,1,0:T(8,128)(2,1)S(1)}, bf16[1024,128]{1,0:T(8,128)(2,1)S(1)}) custom-call(bf16[16,64,128]{2,1,0:T(8,128)(2,1)S(1)} %all-to-all-done.left_in, bf16[16,64,128]{2,1,0:T(8,128)(2,1)S(1)} %all-to-all-done.1.right_in, ...), custom_call_target="tpu_custom_call" | custom-call | tf_op jit(solution)/shard_map/pair_tile/pallas_call | solution.py:210
  77.2 19.8 %all_to_all.35 = bf16[16,128,128]{2,1,0:T(8,128)(2,1)S(1)} all-to-all(bf16[16,128,128]{2,1,0:T(8,128)(2,1)S(1)} %pad_maximum_fusion), channel_id=1, replica_groups=mesh['row'=8,'col'=16,'seq'=2] {'row','seq'}, dimensions={0} | all-to-all | bytes 1048576 | tf_op jit(solution)/shard_map/all_to_all | solution.py:237
  97.0 0.1 reduce_sum.48
  97.1 0.7 pad_maximum_fusion.1
  97.8 8.5 %all-to-all-start.3 = ((bf16[16,68,128]{2,1,0:T(8,128)(2,1)}), bf16[16,68,128]{2,1,0:T(8,128)(2,1)S(1)}, u32[]{:S(2)}, u32[]{:S(2)}) async-start(bf16[16,68,128]{2,1,0:T(8,128)(2,1)} %pad_maximum_fusion.1), calls=%async_computation.3 | async-start | bytes 589824 | tf_op jit(solution)/shard_map/all_to_all | solution.py:241
  106.3 5.3 %collective-permute-start.3 = (bf16[64,128]{1,0:T(8,128)(2,1)S(1)}, bf16[64,128]{1,0:T(8,128)(2,1)S(1)}, u32[]{:S(2)}, u32[]{:S(2)}) collective-permute-start(bf16[64,128]{1,0:T(8,128)(2,1)S(1)} %get-tuple-element.25), channel_id=1, source_target_pairs={{0,0},{32,2},{64,4},{96,6},{128,8},{160,10},{192,12},{224,14},{2,1... | collective-permute-start | bytes 49160 | tf_op jit(solution)/shard_map/ppermute | solution.py:247
  111.7 2.5 %all-to-all-done.3 = bf16[16,68,128]{2,1,0:T(8,128)(2,1)S(1)} async-done(((bf16[16,68,128]{2,1,0:T(8,128)(2,1)}), bf16[16,68,128]{2,1,0:T(8,128)(2,1)S(1)}, u32[]{:S(2)}, u32[]{:S(2)}) %all-to-all-start.3) | async-done | bytes 278560 | tf_op jit(solution)/shard_map/all_to_all | solution.py:241
  114.2 0.1 reduce_sum.49
  114.2 0.0 copy-start.4
  114.3 0.7 collective-permute-start.2
  114.9 0.0 collective-permute-done.3.right_ref
  115.0 0.0 collective-permute-done.2.left_ref
  115.0 1.3 finish.1
  116.2 15.1 %all-to-all-start.4 = ((bf16[16,8,128]{2,1,0:T(8,128)(2,1)}), bf16[16,8,128]{2,1,0:T(8,128)(2,1)S(1)}, u32[]{:S(2)}, u32[]{:S(2)}) async-start(bf16[16,8,128]{2,1,0:T(8,128)(2,1)} %bitcast.12), calls=%async_computation.4 | async-start | bytes 65536 | tf_op jit(solution)/shard_map/all_to_all | solution.py:261
  131.3 0.0 copy-done.4
  131.4 0.0 slice-start
  131.4 7.3 %all-to-all-done.4 = bf16[16,8,128]{2,1,0:T(8,128)(2,1)S(1)} async-done(((bf16[16,8,128]{2,1,0:T(8,128)(2,1)}), bf16[16,8,128]{2,1,0:T(8,128)(2,1)S(1)}, u32[]{:S(2)}, u32[]{:S(2)}) %all-to-all-start.4) | async-done | bytes 32800 | tf_op jit(solution)/shard_map/all_to_all | solution.py:261
  138.7 0.0 slice-done
  138.7 12.1 %all_to_all.36 = bf16[16,12,128]{2,1,0:T(8,128)(2,1)S(1)} all-to-all(bf16[16,12,128]{2,1,0:T(8,128)(2,1)S(1)} %broadcast_in_dim.14), channel_id=1, replica_groups=mesh['row'=8,'col'=16,'seq'=2] {'col'}, dimensions={0} | all-to-all | bytes 98304 | tf_op jit(solution)/shard_map/all_to_all | solution.py:202
  151.0 16.5 %all_to_all.37 = bf16[16,72,128]{2,1,0:T(8,128)(2,1)S(1)} all-to-all(bf16[16,72,128]{2,1,0:T(8,128)(2,1)S(1)} %broadcast_in_dim.15), channel_id=1, replica_groups=mesh['row'=8,'col'=16,'seq'=2] {'row','seq'}, dimensions={0} | all-to-all | bytes 589824 | tf_op jit(solution)/shard_map/all_to_all | solution.py:202
  167.5 0.8 slice.59
  168.4 0.6 fusion.2
  169.0 0.6 reshape.65
  (14 shorter events, 0.2 us)
Async XLA Ops:
  0.6 1.5 copy-start.1
  2.6 0.7 collective-permute-start
  4.1 26.2 %all-to-all-start = ((bf16[16,64,128]{2,1,0:T(8,128)(2,1)}), bf16[16,64,128]{2,1,0:T(8,128)(2,1)S(1)}, u32[]{:S(2)}, u32[]{:S(2)}) async-start(bf16[16,64,128]{2,1,0:T(8,128)(2,1)} %broadcast_in_dim.12), calls=%async_computation | async-start | bytes 524288 | tf_op jit(solution)/shard_map/all_to_all | solution.py:202
  22.4 7.9 %collective-permute-start.1 = (bf16[64,128]{1,0:T(8,128)(2,1)S(1)}, bf16[64,128]{1,0:T(8,128)(2,1)S(1)}, u32[]{:S(2)}, u32[]{:S(2)}) collective-permute-start(bf16[64,128]{1,0:T(8,128)(2,1)S(1)} %get-tuple-element.14), channel_id=1, source_target_pairs={{0,0},{2,32},{4,64},{6,96},{8,128},{10,160},{12,192},{14,224},{16,... | collective-permute-start | bytes 49160 | tf_op jit(solution)/shard_map/ppermute | solution.py:199
  30.3 11.8 %copy-start.3 = (bf16[1024,128]{1,0:T(8,128)(2,1)S(1)}, bf16[1024,128]{1,0:T(8,128)(2,1)}, u32[]{:S(2)}) copy-start(bf16[1024,128]{1,0:T(8,128)(2,1)} %param.9) | copy-start | bytes 786436
  31.1 22.4 %copy-start = (bf16[64,64,128]{2,1,0:T(8,128)(2,1)S(1)}, bf16[64,64,128]{2,1,0:T(8,128)(2,1)}, u32[]{:S(2)}) copy-start(bf16[64,64,128]{2,1,0:T(8,128)(2,1)} %cot_ref.1) | copy-start | bytes 3145732
  31.1 22.4 %all-to-all-start.1 = ((bf16[16,64,128]{2,1,0:T(8,128)(2,1)}), bf16[16,64,128]{2,1,0:T(8,128)(2,1)S(1)}, u32[]{:S(2)}, u32[]{:S(2)}) async-start(bf16[16,64,128]{2,1,0:T(8,128)(2,1)} %broadcast_in_dim.13), calls=%async_computation.1 | async-start | bytes 524288 | tf_op jit(solution)/shard_map/all_to_all | solution.py:202
  53.5 0.7 copy-start.2
  97.8 16.4 %all-to-all-start.3 = ((bf16[16,68,128]{2,1,0:T(8,128)(2,1)}), bf16[16,68,128]{2,1,0:T(8,128)(2,1)S(1)}, u32[]{:S(2)}, u32[]{:S(2)}) async-start(bf16[16,68,128]{2,1,0:T(8,128)(2,1)} %pad_maximum_fusion.1), calls=%async_computation.3 | async-start | bytes 589824 | tf_op jit(solution)/shard_map/all_to_all | solution.py:241
  106.3 8.6 %collective-permute-start.3 = (bf16[64,128]{1,0:T(8,128)(2,1)S(1)}, bf16[64,128]{1,0:T(8,128)(2,1)S(1)}, u32[]{:S(2)}, u32[]{:S(2)}) collective-permute-start(bf16[64,128]{1,0:T(8,128)(2,1)S(1)} %get-tuple-element.25), channel_id=1, source_target_pairs={{0,0},{32,2},{64,4},{96,6},{128,8},{160,10},{192,12},{224,14},{2,1... | collective-permute-start | bytes 49160 | tf_op jit(solution)/shard_map/ppermute | solution.py:247
  114.2 17.1 %copy-start.4 = (bf16[68,128]{1,0:T(8,128)(2,1)}, bf16[68,128]{1,0:T(8,128)(2,1)S(1)}, u32[]{:S(2)}) copy-start(bf16[68,128]{1,0:T(8,128)(2,1)S(1)} %reduce_sum.49) | copy-start | bytes 52228
  114.3 0.7 collective-permute-start.2
  116.2 22.4 %all-to-all-start.4 = ((bf16[16,8,128]{2,1,0:T(8,128)(2,1)}), bf16[16,8,128]{2,1,0:T(8,128)(2,1)S(1)}, u32[]{:S(2)}, u32[]{:S(2)}) async-start(bf16[16,8,128]{2,1,0:T(8,128)(2,1)} %bitcast.12), calls=%async_computation.4 | async-start | bytes 65536 | tf_op jit(solution)/shard_map/all_to_all | solution.py:261
  131.4 7.3 %slice-start = ((bf16[68,128]{1,0:T(8,128)(2,1)}), bf16[4,128]{1,0:T(4,128)(2,1)S(1)}, s32[]{:S(2)}) async-start(bf16[68,128]{1,0:T(8,128)(2,1)} %copy-done.4), calls=%async_computation.7 | async-start | bytes 2048 | tf_op jit(solution)/shard_map/slice | solution.py:245

commit v2 on v1

v2 whole, which is shorter than its diff:
```python
import jax
import jax.numpy as jnp
from jax import lax
from jax.experimental import pallas as pl
from jax.experimental.pallas import tpu as pltpu
from jax.sharding import Mesh, PartitionSpec as P

F32 = jnp.float32
BF16 = jnp.bfloat16
LANES = 128
CP = 32
SEQ_HALF = 32
EPS = 1e-05


def dot(a, b, dims):
    return lax.dot_general(a, b, ((dims[:1], dims[1:]), ((), ())), preferred_element_type=F32)


def params(mib):
    return pltpu.CompilerParams(vmem_limit_bytes=mib << 20)


def normalize(x_ref, rows_ref):
    rows = x_ref[...].astype(F32).reshape(256, 256)
    halves = []
    for h in range(2):
        rows_ref[h] = rows[:, h * 128 : h * 128 + 128]
        halves.append(
            jnp.concatenate([rows_ref[h, pl.ds(i, SEQ_HALF, stride=8), :] for i in range(8)], axis=0)
        )
    values = jnp.concatenate(halves, axis=1)
    center = values - jnp.mean(values, axis=1, keepdims=True)
    invstd = lax.rsqrt(jnp.mean(center * center, axis=1, keepdims=True) + EPS)
    return center * invstd, invstd


def project_kernel(x_ref, left_w, right_w, left_ref, right_ref, normed_ref, rows_ref, block_ref):
    scaled, _ = normalize(x_ref, rows_ref)
    normed = scaled.astype(BF16)
    normed_ref[...] = normed
    left = dot(left_w[...], normed, (1, 1))
    left_ref[0:32, :] = left[:, 0:128].astype(BF16)
    left_ref[32:64, :] = left[:, 128:256].astype(BF16)
    right = dot(right_w[...], normed, (1, 1))
    for half in range(2):
        rows_ref[0, 0:32, :] = right[:, half * 128 : half * 128 + 128]
        rows = [rows_ref[0, pl.ds(k, 8, stride=4), :] for k in range(4)]
        for j in range(4):
            block_ref[half * 32 + j * 8 : half * 32 + j * 8 + 8, :] = jnp.concatenate(
                [rows[k][:, j * 32 : j * 32 + 32] for k in range(4)], axis=1
            )
    right_ref[...] = jnp.concatenate(
        [block_ref[pl.ds(h, 8, stride=8), :] for h in range(8)], axis=0
    ).astype(BF16)


def pair_kernel(
    place_ref, left_in, right_own, right_other, cot_ref, w_scaled_ref, w_turned_ref, bias_ref,
    pair_ref, left_out, keep_out, send_out,
    gathered, spread, left_ref, left_t_ref, grad, outer, left_sum, right_sum, wout_sum, wout_rows,
):
    core = place_ref[0]
    lane = lax.broadcasted_iota(jnp.int32, (64, LANES), 1)
    low = lax.broadcasted_iota(jnp.int32, (32, LANES), 1) < 64
    for b in range(8):
        for half in range(2):
            left_ref[b * 64 : b * 64 + 64, half * 128 : half * 128 + 128] = left_in[half * 8 + b]
    left_t_ref[...] = left_ref[...].astype(F32).T.astype(BF16)
    for z in range(4):
        for half in range(2):
            gathered[(z * 2 + core) * 2 + half] = right_own[z * 2 + half].astype(F32)
            gathered[(z * 2 + 1 - core) * 2 + half] = right_other[z * 2 + half].astype(F32)
    for h in range(8):
        for half in range(2):
            tile = jnp.concatenate(
                [gathered[r * 2 + half, h * 8 : h * 8 + 8, :] for r in range(8)], axis=0
            )
            turned = [tile] + [pltpu.roll(tile, k * 32, 1) for k in range(1, 4)]
            for d in range(4):
                for i in range(4):
                    spread[
                        h, d * 256 + i * 64 : d * 256 + i * 64 + 64, half * 128 : half * 128 + 128
                    ] = jnp.where(lane // 32 == i, turned[(i - d) % 4], 0.0).astype(BF16)

    for i in range(16):
        cot = cot_ref[i * 4 : i * 4 + 4].reshape(256, LANES)
        for h in range(8):
            piece = dot(w_scaled_ref[h * 128 : h * 128 + 128, :], cot, (1, 1)).astype(BF16)
            for d in range(4):
                grad[h, i * 32 : i * 32 + 32, d * 256 : d * 256 + 256] = piece[d * 32 : d * 32 + 32]

    for h in range(8):
        part = dot(grad[h], spread[h], (1, 0))
        left_sum[...] = part if h == 0 else left_sum[...] + part
        for half in range(2):
            parts = []
            part = dot(left_t_ref[half * 128 : half * 128 + 128, :], grad[h], (1, 0))
            for d in range(4):
                lo = part[:, d * 256 : d * 256 + 128]
                hi = part[:, d * 256 + 128 : d * 256 + 256]
                parts.append(
                    jnp.where(low, lo[0:32], lo[32:64]) + jnp.where(low, hi[64:96], hi[96:128])
                )
            turned = jnp.concatenate(parts, axis=0).T
            total = turned[0:64] + turned[64:128]
            for r in range(8):
                right_sum[r * 2 + half, h * 8 : h * 8 + 8, :] = total[r * 8 : r * 8 + 8]
    for b in range(8):
        for half in range(2):
            left_out[half * 8 + b] = left_sum[
                b * 64 : b * 64 + 64, half * 128 : half * 128 + 128
            ].astype(BF16)

    left_ref[...] = (left_ref[...].astype(F32) * (1.0 / 64.0)).astype(BF16)
    for h in range(8):
        for d in range(4):
            piece = dot(left_ref[...], spread[h, d * 256 : d * 256 + 256, :], (1, 1)).astype(BF16)
            first = h * 128 + d * 32
            outer[:, first : first + 32, :] = piece.reshape(16, 32, 256)

    for i in range(16):
        cot = cot_ref[i * 4 : i * 4 + 4].reshape(256, LANES)
        tile = outer[i]
        turned = dot(w_turned_ref[...], tile, (1, 0))
        pair_ref[i * 4 : i * 4 + 4] = (
            (turned.T + bias_ref[...]).astype(BF16).reshape(4, 64, LANES)
        )
        part = dot(tile, cot, (1, 0))
        wout_sum[...] = part if i == 0 else wout_sum[...] + part
    for t in range(16):
        for q in range(4):
            wout_rows[pl.ds(t * 64 + q, 16, stride=4), :] = wout_sum[
                pl.ds(((t % 8) * 4 + q) * 32 + t // 8, 16, stride=2), :
            ]
    for z in range(4):
        for half in range(2):
            for out, owner in ((keep_out, core), (send_out, 1 - core)):
                b = (z * 2 + owner) * 2 + half
                out[z * 2 + half, 0:64] = right_sum[b].astype(out.dtype)
                out[z * 2 + half, 64:128] = wout_rows[
                    pl.ds(pl.multiple_of(b * 64, 64), 64), :
                ].astype(out.dtype)


def turn_grads(left, right, rows_ref, turn_ref):
    rows_ref[...] = right
    rows = [rows_ref[pl.ds(j, 8, stride=8), :] for j in range(8)]
    for half in range(2):
        for k in range(4):
            turn_ref[half, pl.ds(k, 8, stride=4), :] = jnp.concatenate(
                [rows[half * 4 + j][:, k * 32 : k * 32 + 32] for j in range(4)], axis=1
            )
    right = jnp.concatenate([turn_ref[0], turn_ref[1]], axis=1).astype(BF16)
    left = jnp.concatenate([left[0:32], left[32:64]], axis=1).astype(BF16)
    return left, right


def weights_kernel(left_ref, right_ref, wout_ref, normed_ref, next_ref, rows_ref, turn_ref):
    left, right = turn_grads(
        left_ref[...].astype(F32), right_ref[...].astype(F32), rows_ref, turn_ref
    )
    wout = wout_ref[...].astype(F32)
    total = dot(jnp.concatenate([left, right], axis=0), normed_ref[...], (1, 0)).astype(BF16)
    for half in range(2):
        for b in range(8):
            next_ref[half * 8 + b, 0:8, :] = total[b * 8 : b * 8 + 8, half * 128 : half * 128 + 128]
    for b in range(16):
        next_ref[b, 8:12, :] = wout[b * 4 : b * 4 + 4].astype(BF16)
    next_ref[:, 12:16, :] = jnp.zeros((16, 4, LANES), BF16)


def align_kernel(x_ref, left_w, right_w, left_ref, right_ref, align_ref, rows_ref, block_ref, turn_ref):
    scaled, invstd = normalize(x_ref, rows_ref)
    left, right = turn_grads(
        left_ref[...].astype(F32), right_ref[...].astype(F32), block_ref, turn_ref
    )
    normed_grad = dot(left, left_w[...], (0, 0)) + dot(right, right_w[...], (0, 0))
    mean_grad = jnp.mean(normed_grad, axis=1, keepdims=True)
    mean_cross = jnp.mean(normed_grad * scaled, axis=1, keepdims=True)
    result = invstd * (normed_grad - mean_grad - scaled * mean_cross)
    for h in range(2):
        for i in range(8):
            rows_ref[h, pl.ds(i, SEQ_HALF, stride=8), :] = result[
                i * 32 : i * 32 + 32, h * 128 : h * 128 + 128
            ]
        align_ref[:, h * 128 : h * 128 + 128] = rows_ref[h]


def last_kernel(in_ref, wout_ref, left_ref, right_ref):
    for b in range(16):
        wout_ref[b * 64 : b * 64 + 64, :] = in_ref[b, 0:64].astype(F32) * (1.0 / 1024.0)
    for half in range(2):
        for out, first in ((left_ref, 0), (right_ref, 4)):
            for b in range(4):
                out[b * 8 : b * 8 + 8, half * 128 : half * 128 + 128] = in_ref[
                    half * 8 + first + b, 64:72
                ].astype(F32) * (1.0 / 1024.0)


def body(alignment, left_weight, right_weight, out_weight, out_bias, cotangent):
    rows_n, cols_n, seq_n = 8, lax.axis_size("col"), lax.axis_size("seq")
    row, column = ("z", "core"), ("z", "seq")
    to_left = [
        (c * seq_n + s, c * seq_n + s if c // 8 == s else (c ^ 8) * seq_n + 1 - s)
        for c in range(cols_n)
        for s in range(seq_n)
    ]
    to_right = [
        (r * cols_n + c, (c % 8) * cols_n + 2 * r + c // 8) for r in range(rows_n) for c in range(cols_n)
    ]
    back = [(b, a) for a, b in to_right]
    struct = jax.ShapeDtypeStruct
    vmem = pltpu.VMEM
    left_w, right_w = left_weight.T, right_weight.T
    w_rows = out_weight.reshape(CP, CP, LANES).transpose(1, 0, 2).reshape(CP * CP, LANES)
    w_scaled = (w_rows.astype(F32) * (1.0 / 64.0)).astype(BF16)
    w_turned = w_rows.T
    place = jnp.stack([lax.axis_index("core"), lax.axis_index("seq")]).astype(jnp.int32)
    smem = pl.BlockSpec(memory_space=pltpu.SMEM)

    def exchange(value, axes):
        return lax.all_to_all(value, axes, 0, 0, tiled=True)

    def gather(value, axes, count):
        return exchange(jnp.broadcast_to(value, (count,) + value.shape), axes)

    def total(value):
        return jnp.sum(value.astype(F32), axis=0).astype(BF16)

    def other_core(value):
        return lax.ppermute(value, "core", [(0, 1), (1, 0)])

    def cost(flops, nbytes):
        return pl.CostEstimate(flops=flops, bytes_accessed=nbytes, transcendentals=0)

    def in_hbm(value):
        return pltpu.with_memory_space_constraint(value, pltpu.HBM)

    block = struct((64, LANES), BF16)
    left_block, right_block, normed = pl.pallas_call(
        project_kernel,
        out_shape=(block, block, struct((256, 256), BF16)),
        scratch_shapes=[vmem((2, 256, LANES), F32), vmem((64, LANES), F32)],
        compiler_params=params(8),
        name="project",
    )(in_hbm(alignment), in_hbm(left_w), in_hbm(right_w))

    right_block = lax.ppermute(right_block, row + ("col",), to_right)
    left_block = lax.ppermute(left_block, ("col", "seq"), to_left)
    right_own = gather(right_block, column, 8)
    left_all = gather(left_block, "col", 16)
    right_other = other_core(right_own)

    vm = pl.BlockSpec(memory_space=vmem)
    pair, left_part, keep, send = pl.pallas_call(
        pair_kernel,
        in_specs=[smem] + [vm] * 7,
        out_shape=(
            struct((64, 64, LANES), BF16),
            struct((16, 64, LANES), BF16),
            struct((8, 128, LANES), F32),
            struct((8, 128, LANES), BF16),
        ),
        scratch_shapes=[
            vmem((16, 64, LANES), F32),
            vmem((8, 1024, 256), BF16),
            vmem((512, 256), BF16),
            vmem((256, 512), BF16),
            vmem((8, 512, 1024), BF16),
            vmem((16, 1024, 256), BF16),
            vmem((512, 256), F32),
            vmem((16, 64, LANES), F32),
            vmem((1024, LANES), F32),
            vmem((1024, LANES), F32),
        ],
        compiler_params=params(40),
        cost_estimate=cost(8 << 30, 6 << 20),
        name="pair_tile",
    )(
        place,
        left_all,
        right_own,
        right_other,
        cotangent,
        w_scaled,
        w_turned,
        out_bias.reshape(1, LANES),
    )

    left_back = exchange(left_part, "col")
    right_send = (keep + other_core(send).astype(F32)).astype(BF16)
    right_send, left_back = lax.optimization_barrier((right_send, left_back))
    left_grad = lax.ppermute(total(left_back), ("col", "seq"), to_left)
    first = total(exchange(right_send, column))
    right_grad = lax.ppermute(first[:64], row + ("col",), back)
    stage = pl.pallas_call(
        weights_kernel,
        out_shape=struct((16, 16, LANES), BF16),
        scratch_shapes=[vmem((64, LANES), F32), vmem((2, 32, LANES), F32)],
        compiler_params=params(8),
        name="weight_grads",
    )(left_grad, right_grad, first[64:], normed)

    stage = gather(total(exchange(stage, "col")), ("z", "core", "seq"), 16)
    last = gather(
        jnp.concatenate(
            [stage[:, 8:12].reshape(64, LANES), total(stage[:, :8]), jnp.zeros((8, LANES), BF16)], axis=0
        ),
        "col",
        16,
    )
    align_grad = pl.pallas_call(
        align_kernel,
        out_shape=struct((256, 256), F32),
        scratch_shapes=[vmem((2, 256, LANES), F32), vmem((64, LANES), F32), vmem((2, 32, LANES), F32)],
        compiler_params=params(8),
        cost_estimate=cost(1 << 24, 1 << 20),
        name="align",
    )(in_hbm(alignment), left_w, right_w, left_grad, right_grad)
    wout_grad, left_weight_grad, right_weight_grad = pl.pallas_call(
        last_kernel,
        out_shape=(struct((1024, LANES), F32), struct((32, 256), F32), struct((32, 256), F32)),
        compiler_params=params(8),
        name="last",
    )(last)
    return (
        pair,
        align_grad.reshape(alignment.shape),
        left_weight_grad.T,
        right_weight_grad.T,
        wout_grad,
    )


def solution(mesh):
    z = mesh.shape["row"] // 2
    fine = Mesh(
        mesh.devices.reshape(z, 2, mesh.shape["col"], mesh.shape["seq"]), ("z", "core", "col", "seq")
    )
    row = ("z", "core")
    tiles, blocks = P(row + ("seq",), "col", None), P("seq", row + ("col",), None)
    return jax.shard_map(
        body,
        mesh=fine,
        in_specs=(blocks, P(), P(), P(), P(), tiles),
        out_specs=(tiles, blocks, P(), P(), P()),
        check_vma=False,
    )
```

time: 170 us -> 144 us (0.85)
  blocking collectives: 48.5 us -> 13.6 us
  waiting for transfers between devices: 21.7 us -> 39.5 us
  Pallas kernels: 24.7 us -> 18.9 us
    all_to_all x3 -> x1, blocking collectives: 48.5 us -> 13.6 us  [exchange(): return lax.all_to_all(value, axes, 0, 0, tiled=True)]
    all_to_all x4 -> x6, waiting for transfers between devices: 20.8 us -> 36.9 us  [exchange(): return lax.all_to_all(value, axes, 0, 0, tiled=True)]
    all_to_all x4 -> x6, starting transfers between devices: 53 us -> 42.4 us  [exchange(): return lax.all_to_all(value, axes, 0, 0, tiled=True)]
    ppermute x3 -> x5, starting transfers between devices: 13 us -> 22 us  [the longest x2 10.1 us: other_core(): return lax.ppermute(value, 'core', [(0, 1), (1, 0)])]
    pallas_call x3 -> x5, Pallas kernels: 24.7 us -> 18.9 us  [the longest x1 14.2 us: body(): pl.pallas_call(pair_kernel, in_specs=[smem] + [vm] * 7, out_shape=(struct...]
  transfers between devices with their start and end apart: 8 -> 12, of which waited for: 4 -> 8; matrix products, arithmetic and copies ran while one was open for 0% -> 1% of each run, Pallas kernels for 0% -> 1%
where the time goes in v2:
time: 144 us; the launch traced here: 143 us
  starting transfers between devices  65.1 us (45%)
  waiting for transfers between devices  39.5 us (27%)
  Pallas kernels  18.9 us (13%)
  blocking collectives  13.6 us (9%)
  local copies, waits for them, and re-layouts  3.85 us (3%)
    all_to_all x6, starting transfers between devices, exchange(): return lax.all_to_all(value, axes, 0, 0, tiled=True)  42.4 us
    all_to_all x6, waiting for transfers between devices, exchange(): return lax.all_to_all(value, axes, 0, 0, tiled=True)  36.9 us
    pallas_call x1, Pallas kernels, body(): pl.pallas_call(pair_kernel, in_specs=[smem] + [vm] * 7, out_shape=(struct...  14.2 us
    all_to_all x1, blocking collectives, exchange(): return lax.all_to_all(value, axes, 0, 0, tiled=True)  13.6 us
    ppermute x2, starting transfers between devices, other_core(): return lax.ppermute(value, 'core', [(0, 1), (1, 0)])  10.1 us
    ppermute x1, starting transfers between devices, body(): right_block = lax.ppermute(right_block, row + ('col',), to_right)  6.04 us
    ppermute x1, starting transfers between devices, body(): right_grad = lax.ppermute(first[:64], row + ('col',), back)  5.23 us
  transfers between devices with their start and end apart: 12, of which 8 were waited for; matrix products, arithmetic and copies ran while one was open for 1% of the time, Pallas kernels for 1%

profile of v2, /device:TPU:1, one launch (start us, length us, event | category | flops | bytes accessed | tf_op | source)
XLA Modules:
  0.0 142.9 jit_solution(2484240433077714582)
XLA Ops:
  0.6 0.0 copy-start.4
  0.6 1.5 %project.1 = (bf16[64,128]{1,0:T(8,128)(2,1)S(1)}, bf16[64,128]{1,0:T(8,128)(2,1)S(1)}, bf16[256,256]{1,0:T(8,128)(2,1)S(1)}) custom-call(bf16[32,8,256]{2,1,0:T(8,128)(2,1)} %x_ref.3, bf16[32,256]{1,0:T(8,128)(2,1)} %bitcast.16, bf16[32,256]{1,0:T(8,128)(2,1)} %bitcast.18), custom_call_target="tpu_custom_call" | custom-call | tf_op jit(solution)/shard_map/project/pallas_call | solution.py:241
  2.1 6.0 %collective-permute-start.1 = (bf16[64,128]{1,0:T(8,128)(2,1)S(1)}, bf16[64,128]{1,0:T(8,128)(2,1)S(1)}, u32[]{:S(2)}, u32[]{:S(2)}) collective-permute-start(bf16[64,128]{1,0:T(8,128)(2,1)S(1)} %get-tuple-element.18), channel_id=1, source_target_pairs={{0,0},{2,32},{4,64},{6,96},{8,128},{10,160},{12,192},{14,224},{16,... | collective-permute-start | bytes 49160 | tf_op jit(solution)/shard_map/ppermute | solution.py:249
  8.2 0.8 collective-permute-done.1
  9.0 0.7 broadcast_in_dim.16
  9.7 10.8 %all-to-all-start.1 = ((bf16[8,64,128]{2,1,0:T(8,128)(2,1)}), bf16[8,64,128]{2,1,0:T(8,128)(2,1)S(1)}, u32[]{:S(2)}, u32[]{:S(2)}) async-start(bf16[8,64,128]{2,1,0:T(8,128)(2,1)} %broadcast_in_dim.16), calls=%async_computation.1 | async-start | bytes 262144 | tf_op jit(solution)/shard_map/all_to_all | solution.py:223
  20.5 0.7 collective-permute-start
  21.2 0.0 copy-done.4
  21.2 0.1 copy.14
  21.3 0.0 copy-start.2
  21.3 0.0 collective-permute-done
  21.3 5.9 %all-to-all-done.1.right_own = bf16[8,64,128]{2,1,0:T(8,128)(2,1)S(1)} async-done(((bf16[8,64,128]{2,1,0:T(8,128)(2,1)}), bf16[8,64,128]{2,1,0:T(8,128)(2,1)S(1)}, u32[]{:S(2)}, u32[]{:S(2)}) %all-to-all-start.1) | async-done | bytes 131104 | tf_op jit(solution)/shard_map/all_to_all | solution.py:223
  27.3 0.8 broadcast_in_dim.15
  28.0 11.2 %all-to-all-start = ((bf16[16,64,128]{2,1,0:T(8,128)(2,1)}), bf16[16,64,128]{2,1,0:T(8,128)(2,1)S(1)}, u32[]{:S(2)}, u32[]{:S(2)}) async-start(bf16[16,64,128]{2,1,0:T(8,128)(2,1)} %broadcast_in_dim.15), calls=%async_computation | async-start | bytes 524288 | tf_op jit(solution)/shard_map/all_to_all | solution.py:223
  39.3 4.5 %collective-permute-start.2 = (bf16[8,64,128]{2,1,0:T(8,128)(2,1)S(1)}, bf16[8,64,128]{2,1,0:T(8,128)(2,1)S(1)}, u32[]{:S(2)}, u32[]{:S(2)}) collective-permute-start(bf16[8,64,128]{2,1,0:T(8,128)(2,1)S(1)} %all-to-all-done.1.right_own), channel_id=1, source_target_pairs={{0,32},{32,0},{1,33},{33,1},{2,34},{34,2},{3,35},{35,3},{4,36},{36... | collective-permute-start | bytes 393224 | tf_op jit(solution)/shard_map/ppermute | solution.py:232
  43.8 0.1 multiply_convert_fusion.w_scaled_ref
  43.9 0.1 copy.15
  44.0 0.1 pad_add_fusion.place_ref
  44.1 2.7 %all-to-all-done.left_in = bf16[16,64,128]{2,1,0:T(8,128)(2,1)S(1)} async-done(((bf16[16,64,128]{2,1,0:T(8,128)(2,1)}), bf16[16,64,128]{2,1,0:T(8,128)(2,1)S(1)}, u32[]{:S(2)}, u32[]{:S(2)}) %all-to-all-start) | async-done | bytes 262176 | tf_op jit(solution)/shard_map/all_to_all | solution.py:223
  46.8 0.0 collective-permute-done.2.right_other
  46.8 0.0 copy-done.2
  46.8 0.6 copy-done.3
  47.5 14.2 %pair_tile.1 = (bf16[64,64,128]{2,1,0:T(8,128)(2,1)}, bf16[16,64,128]{2,1,0:T(8,128)(2,1)}, f32[8,128,128]{2,1,0:T(8,128)S(1)}, bf16[8,128,128]{2,1,0:T(8,128)(2,1)S(1)}) custom-call(s32[2]{0:T(128)S(1)} %pad_add_fusion.place_ref, bf16[16,64,128]{2,1,0:T(8,128)(2,1)S(1)} %all-to-all-done.left_in, bf16[8,64,128]{2,1,0:T(8,128)(2,1)S(1)} %all-to-all-done.1.right_own, ...), custom_call_target="tpu_custom_call" | custom-call | flops 8589934592 | bytes 6291456 | tf_op jit(solution)/shard_map/pair_tile/pallas_call | solution.py:256
  61.7 5.6 %collective-permute-start.3 = (bf16[8,128,128]{2,1,0:T(8,128)(2,1)S(1)}, bf16[8,128,128]{2,1,0:T(8,128)(2,1)S(1)}, u32[]{:S(2)}, u32[]{:S(2)}) collective-permute-start(bf16[8,128,128]{2,1,0:T(8,128)(2,1)S(1)} %get-tuple-element.21), channel_id=1, source_target_pairs={{0,32},{32,0},{1,33},{33,1},{2,34},{34,2},{3,35},{35,3},{4,36},{36... | collective-permute-start | bytes 786440 | tf_op jit(solution)/shard_map/ppermute | solution.py:232
  67.3 3.5 %all-to-all-start.2 = ((bf16[16,64,128]{2,1,0:T(8,128)(2,1)}), bf16[16,64,128]{2,1,0:T(8,128)(2,1)S(1)}, u32[]{:S(2)}, u32[]{:S(2)}) async-start(bf16[16,64,128]{2,1,0:T(8,128)(2,1)} %get-tuple-element.22), calls=%async_computation.2 | async-start | bytes 524288 | tf_op jit(solution)/shard_map/all_to_all | solution.py:223
  70.8 0.0 collective-permute-done.3
  70.8 0.8 add_convert_fusion
  71.6 7.7 %all-to-all-done.2 = bf16[16,64,128]{2,1,0:T(8,128)(2,1)S(1)} async-done(((bf16[16,64,128]{2,1,0:T(8,128)(2,1)}), bf16[16,64,128]{2,1,0:T(8,128)(2,1)S(1)}, u32[]{:S(2)}, u32[]{:S(2)}) %all-to-all-start.2) | async-done | bytes 262176 | tf_op jit(solution)/shard_map/all_to_all | solution.py:223
  79.3 4.8 %all-to-all-start.3 = ((bf16[8,128,128]{2,1,0:T(8,128)(2,1)}), bf16[8,128,128]{2,1,0:T(8,128)(2,1)S(1)}, u32[]{:S(2)}, u32[]{:S(2)}) async-start(bf16[8,128,128]{2,1,0:T(8,128)(2,1)} %add_convert_fusion), calls=%async_computation.3 | async-start | bytes 524288 | tf_op jit(solution)/shard_map/all_to_all | solution.py:223
  84.2 0.7 collective-permute-start.4
  84.9 6.4 %all-to-all-done.3 = bf16[8,128,128]{2,1,0:T(8,128)(2,1)S(1)} async-done(((bf16[8,128,128]{2,1,0:T(8,128)(2,1)}), bf16[8,128,128]{2,1,0:T(8,128)(2,1)S(1)}, u32[]{:S(2)}, u32[]{:S(2)}) %all-to-all-start.3) | async-done | bytes 262176 | tf_op jit(solution)/shard_map/all_to_all | solution.py:223
  91.4 5.2 %collective-permute-start.5 = (bf16[64,128]{1,0:T(8,128)(2,1)S(1)}, bf16[64,128]{1,0:T(8,128)(2,1)S(1)}, u32[]{:S(2)}, u32[]{:S(2)}) collective-permute-start(bf16[64,128]{1,0:T(8,128)(2,1)S(1)} %get-tuple-element.30), channel_id=1, source_target_pairs={{0,0},{32,2},{64,4},{96,6},{128,8},{160,10},{192,12},{224,14},{2,1... | collective-permute-start | bytes 49160 | tf_op jit(solution)/shard_map/ppermute | solution.py:296
  96.6 0.0 collective-permute-done.4.left_ref
  96.6 1.7 %collective-permute-done.5.right_ref = bf16[64,128]{1,0:T(8,128)(2,1)S(1)} collective-permute-done((bf16[64,128]{1,0:T(8,128)(2,1)S(1)}, bf16[64,128]{1,0:T(8,128)(2,1)S(1)}, u32[]{:S(2)}, u32[]{:S(2)}) %collective-permute-start.5) | collective-permute-done | bytes 16416 | tf_op jit(solution)/shard_map/ppermute | solution.py:296
  98.3 0.2 weight_grads.1
  98.5 13.6 %all_to_all.35 = bf16[16,16,128]{2,1,0:T(8,128)(2,1)S(1)} all-to-all(bf16[16,16,128]{2,1,0:T(8,128)(2,1)S(1)} %weight_grads.1), channel_id=1, replica_groups=mesh['z'=4,'core'=2,'col'=16,'seq'=2] {'col'}, dimensions={0} | all-to-all | bytes 131072 | tf_op jit(solution)/shard_map/all_to_all | solution.py:223
  112.2 0.6 broadcast_in_dim.17
  112.8 8.4 %all-to-all-start.5 = ((bf16[16,16,128]{2,1,0:T(8,128)(2,1)}), bf16[16,16,128]{2,1,0:T(8,128)(2,1)S(1)}, u32[]{:S(2)}, u32[]{:S(2)}) async-start(bf16[16,16,128]{2,1,0:T(8,128)(2,1)} %broadcast_in_dim.17), calls=%async_computation.5 | async-start | bytes 131072 | tf_op jit(solution)/shard_map/all_to_all | solution.py:223
  121.2 0.1 pad.2.clone
  121.3 7.6 %all-to-all-done.5 = bf16[16,16,128]{2,1,0:T(8,128)(2,1)S(1)} async-done(((bf16[16,16,128]{2,1,0:T(8,128)(2,1)}), bf16[16,16,128]{2,1,0:T(8,128)(2,1)S(1)}, u32[]{:S(2)}, u32[]{:S(2)}) %all-to-all-start.5) | async-done | bytes 65568 | tf_op jit(solution)/shard_map/all_to_all | solution.py:223
  128.8 0.1 maximum_maximum_fusion
  128.9 0.8 broadcast_in_dim.19
  129.7 3.7 %all-to-all-start.6 = ((bf16[16,80,128]{2,1,0:T(8,128)(2,1)}), bf16[16,80,128]{2,1,0:T(8,128)(2,1)S(1)}, u32[]{:S(2)}, u32[]{:S(2)}) async-start(bf16[16,80,128]{2,1,0:T(8,128)(2,1)} %broadcast_in_dim.19), calls=%async_computation.6 | async-start | bytes 655360 | tf_op jit(solution)/shard_map/all_to_all | solution.py:223
  133.4 0.0 copy-done
  133.4 0.0 copy-done.1
  133.4 2.1 %align.1 = f32[256,256]{1,0:T(8,128)} custom-call(bf16[32,8,256]{2,1,0:T(8,128)(2,1)} %x_ref.3, bf16[32,256]{1,0:T(8,128)(2,1)S(1)} %bitcast.17, bf16[32,256]{1,0:T(8,128)(2,1)S(1)} %bitcast.19, bf16[64,128]{1,0:T(8,128)(2,1)S(1)} %collective-permute-done.4.left_ref, bf16[64,128]{1,0:T(8,128)(2,1)S(1)} %collective-permute-done.5.right_ref), custom_call_target="tpu_custom_call" | custom-call | flops 16777216 | bytes 1048576 | tf_op jit(solution)/shard_map/align/pallas_call | solution.py:313
  135.5 6.6 %all-to-all-done.6.in_ref = bf16[16,80,128]{2,1,0:T(8,128)(2,1)S(1)} async-done(((bf16[16,80,128]{2,1,0:T(8,128)(2,1)}), bf16[16,80,128]{2,1,0:T(8,128)(2,1)S(1)}, u32[]{:S(2)}, u32[]{:S(2)}) %all-to-all-start.6) | async-done | bytes 327712 | tf_op jit(solution)/shard_map/all_to_all | solution.py:223
  142.1 0.8 last.1
  (10 shorter events, 0.1 us)
Async XLA Ops:
  0.6 20.5 %copy-start.4 = (bf16[1024,128]{1,0:T(8,128)(2,1)S(1)}, bf16[1024,128]{1,0:T(8,128)(2,1)}, u32[]{:S(2)}) copy-start(bf16[1024,128]{1,0:T(8,128)(2,1)} %param.9) | copy-start | bytes 786436
  2.1 6.9 %collective-permute-start.1 = (bf16[64,128]{1,0:T(8,128)(2,1)S(1)}, bf16[64,128]{1,0:T(8,128)(2,1)S(1)}, u32[]{:S(2)}, u32[]{:S(2)}) collective-permute-start(bf16[64,128]{1,0:T(8,128)(2,1)S(1)} %get-tuple-element.18), channel_id=1, source_target_pairs={{0,0},{2,32},{4,64},{6,96},{8,128},{10,160},{12,192},{14,224},{16,... | collective-permute-start | bytes 49160 | tf_op jit(solution)/shard_map/ppermute | solution.py:249
  9.7 17.6 %all-to-all-start.1 = ((bf16[8,64,128]{2,1,0:T(8,128)(2,1)}), bf16[8,64,128]{2,1,0:T(8,128)(2,1)S(1)}, u32[]{:S(2)}, u32[]{:S(2)}) async-start(bf16[8,64,128]{2,1,0:T(8,128)(2,1)} %broadcast_in_dim.16), calls=%async_computation.1 | async-start | bytes 262144 | tf_op jit(solution)/shard_map/all_to_all | solution.py:223
  20.5 0.8 collective-permute-start
  21.3 25.5 %copy-start.2 = (bf16[64,64,128]{2,1,0:T(8,128)(2,1)S(1)}, bf16[64,64,128]{2,1,0:T(8,128)(2,1)}, u32[]{:S(2)}) copy-start(bf16[64,64,128]{2,1,0:T(8,128)(2,1)} %cot_ref.1) | copy-start | bytes 3145732
  28.0 18.8 %all-to-all-start = ((bf16[16,64,128]{2,1,0:T(8,128)(2,1)}), bf16[16,64,128]{2,1,0:T(8,128)(2,1)S(1)}, u32[]{:S(2)}, u32[]{:S(2)}) async-start(bf16[16,64,128]{2,1,0:T(8,128)(2,1)} %broadcast_in_dim.15), calls=%async_computation | async-start | bytes 524288 | tf_op jit(solution)/shard_map/all_to_all | solution.py:223
  39.3 7.5 %collective-permute-start.2 = (bf16[8,64,128]{2,1,0:T(8,128)(2,1)S(1)}, bf16[8,64,128]{2,1,0:T(8,128)(2,1)S(1)}, u32[]{:S(2)}, u32[]{:S(2)}) collective-permute-start(bf16[8,64,128]{2,1,0:T(8,128)(2,1)S(1)} %all-to-all-done.1.right_own), channel_id=1, source_target_pairs={{0,32},{32,0},{1,33},{33,1},{2,34},{34,2},{3,35},{35,3},{4,36},{36... | collective-permute-start | bytes 393224 | tf_op jit(solution)/shard_map/ppermute | solution.py:232
  46.8 0.7 copy-start.3
  61.7 9.1 %collective-permute-start.3 = (bf16[8,128,128]{2,1,0:T(8,128)(2,1)S(1)}, bf16[8,128,128]{2,1,0:T(8,128)(2,1)S(1)}, u32[]{:S(2)}, u32[]{:S(2)}) collective-permute-start(bf16[8,128,128]{2,1,0:T(8,128)(2,1)S(1)} %get-tuple-element.21), channel_id=1, source_target_pairs={{0,32},{32,0},{1,33},{33,1},{2,34},{34,2},{3,35},{35,3},{4,36},{36... | collective-permute-start | bytes 786440 | tf_op jit(solution)/shard_map/ppermute | solution.py:232
  67.3 12.1 %all-to-all-start.2 = ((bf16[16,64,128]{2,1,0:T(8,128)(2,1)}), bf16[16,64,128]{2,1,0:T(8,128)(2,1)S(1)}, u32[]{:S(2)}, u32[]{:S(2)}) async-start(bf16[16,64,128]{2,1,0:T(8,128)(2,1)} %get-tuple-element.22), calls=%async_computation.2 | async-start | bytes 524288 | tf_op jit(solution)/shard_map/all_to_all | solution.py:223
  79.3 12.0 %all-to-all-start.3 = ((bf16[8,128,128]{2,1,0:T(8,128)(2,1)}), bf16[8,128,128]{2,1,0:T(8,128)(2,1)S(1)}, u32[]{:S(2)}, u32[]{:S(2)}) async-start(bf16[8,128,128]{2,1,0:T(8,128)(2,1)} %add_convert_fusion), calls=%async_computation.3 | async-start | bytes 524288 | tf_op jit(solution)/shard_map/all_to_all | solution.py:223
  84.2 12.4 %collective-permute-start.4 = (bf16[64,128]{1,0:T(8,128)(2,1)S(1)}, bf16[64,128]{1,0:T(8,128)(2,1)S(1)}, u32[]{:S(2)}, u32[]{:S(2)}) collective-permute-start(bf16[64,128]{1,0:T(8,128)(2,1)S(1)} %reduce_sum.48), channel_id=1, source_target_pairs={{0,0},{1,16},{2,2},{3,18},{4,4},{5,20},{6,6},{7,22},{8,8},{9,24},{... | collective-permute-start | bytes 49160 | tf_op jit(solution)/shard_map/ppermute | solution.py:294
  91.4 7.0 %collective-permute-start.5 = (bf16[64,128]{1,0:T(8,128)(2,1)S(1)}, bf16[64,128]{1,0:T(8,128)(2,1)S(1)}, u32[]{:S(2)}, u32[]{:S(2)}) collective-permute-start(bf16[64,128]{1,0:T(8,128)(2,1)S(1)} %get-tuple-element.30), channel_id=1, source_target_pairs={{0,0},{32,2},{64,4},{96,6},{128,8},{160,10},{192,12},{224,14},{2,1... | collective-permute-start | bytes 49160 | tf_op jit(solution)/shard_map/ppermute | solution.py:296
  112.8 16.0 %all-to-all-start.5 = ((bf16[16,16,128]{2,1,0:T(8,128)(2,1)}), bf16[16,16,128]{2,1,0:T(8,128)(2,1)S(1)}, u32[]{:S(2)}, u32[]{:S(2)}) async-start(bf16[16,16,128]{2,1,0:T(8,128)(2,1)} %broadcast_in_dim.17), calls=%async_computation.5 | async-start | bytes 131072 | tf_op jit(solution)/shard_map/all_to_all | solution.py:223
  129.7 3.7 %copy-start = (bf16[256,32]{0,1:T(8,128)(2,1)S(1)}, bf16[256,32]{0,1:T(8,128)(2,1)}, u32[]{:S(2)}) copy-start(bf16[256,32]{0,1:T(8,128)(2,1)} %param.7) | copy-start | bytes 49156
  129.7 3.7 %copy-start.1 = (bf16[256,32]{0,1:T(8,128)(2,1)S(1)}, bf16[256,32]{0,1:T(8,128)(2,1)}, u32[]{:S(2)}) copy-start(bf16[256,32]{0,1:T(8,128)(2,1)} %param.8) | copy-start | bytes 49156
  129.7 12.4 %all-to-all-start.6 = ((bf16[16,80,128]{2,1,0:T(8,128)(2,1)}), bf16[16,80,128]{2,1,0:T(8,128)(2,1)S(1)}, u32[]{:S(2)}, u32[]{:S(2)}) async-start(bf16[16,80,128]{2,1,0:T(8,128)(2,1)} %broadcast_in_dim.19), calls=%async_computation.6 | async-start | bytes 655360 | tf_op jit(solution)/shard_map/all_to_all | solution.py:223

commit v3 on v2

v3 whole, which is shorter than its diff:
```python
import jax
import jax.numpy as jnp
from jax import lax
from jax.experimental import pallas as pl
from jax.experimental.pallas import tpu as pltpu
from jax.sharding import Mesh, PartitionSpec as P

F32 = jnp.float32
BF16 = jnp.bfloat16
LANES = 128
CP = 32
SEQ_HALF = 32
EPS = 1e-05


def dot(a, b, dims):
    return lax.dot_general(a, b, ((dims[:1], dims[1:]), ((), ())), preferred_element_type=F32)


def params(mib):
    return pltpu.CompilerParams(vmem_limit_bytes=mib << 20)


def normalize(x_ref, rows_ref):
    rows = x_ref[...].astype(F32).reshape(256, 256)
    halves = []
    for h in range(2):
        rows_ref[h] = rows[:, h * 128 : h * 128 + 128]
        halves.append(
            jnp.concatenate([rows_ref[h, pl.ds(i, SEQ_HALF, stride=8), :] for i in range(8)], axis=0)
        )
    values = jnp.concatenate(halves, axis=1)
    center = values - jnp.mean(values, axis=1, keepdims=True)
    invstd = lax.rsqrt(jnp.mean(center * center, axis=1, keepdims=True) + EPS)
    return center * invstd, invstd


def project_kernel(x_ref, left_w, right_w, both_ref, normed_ref, rows_ref, block_ref):
    scaled, _ = normalize(x_ref, rows_ref)
    normed = scaled.astype(BF16)
    normed_ref[...] = normed
    left = dot(left_w[...], normed, (1, 1))
    left = jnp.concatenate([left[:, 0:128], left[:, 128:256]], axis=0).astype(BF16)
    right = dot(right_w[...], normed, (1, 1))
    for half in range(2):
        rows_ref[0, 0:32, :] = right[:, half * 128 : half * 128 + 128]
        rows = [rows_ref[0, pl.ds(k, 8, stride=4), :] for k in range(4)]
        for j in range(4):
            block_ref[half * 32 + j * 8 : half * 32 + j * 8 + 8, :] = jnp.concatenate(
                [rows[k][:, j * 32 : j * 32 + 32] for k in range(4)], axis=1
            )
    right = jnp.concatenate(
        [block_ref[pl.ds(h, 8, stride=8), :] for h in range(8)], axis=0
    ).astype(BF16)
    for b in range(8):
        both_ref[b, 0:64] = right
        both_ref[b, 64:128] = left


def route_kernel(own_ref, other_ref, out_ref):
    core, upper, z_own = lax.axis_index("core"), lax.axis_index("col") // 8, lax.axis_index("z")
    left = [own_ref[z_own * 2 + half, 64:128] for half in range(2)]
    none = jnp.zeros((LANES, LANES), BF16)
    for c in range(16):
        out_ref[c, 0:64] = left[0]
        out_ref[c, 64:128] = left[1]
    for z in range(4):
        for owner, rights in ((core, own_ref), (1 - core, other_ref)):
            c = (z * 2 + owner) * 2
            out_ref[c + upper, 128:192] = rights[z * 2, 0:64]
            out_ref[c + upper, 192:256] = rights[z * 2 + 1, 0:64]
            out_ref[c + 1 - upper, 128:256] = none


def fill(blocks, left_ref, gathered, spread):
    odd, seq = lax.axis_index("col") % 2, lax.axis_index("seq")
    lane = lax.broadcasted_iota(jnp.int32, (64, LANES), 1)
    for b in range(8):
        for half in range(2):
            left_ref[b * 64 : b * 64 + 64, half * 128 : half * 128 + 128] = blocks[
                seq * 8 + b, half * 64 : half * 64 + 64
            ]
            gathered[b * 2 + half] = blocks[
                odd * 8 + b, 128 + half * 64 : 192 + half * 64
            ].astype(F32)
    for h in range(8):
        for half in range(2):
            tile = jnp.concatenate(
                [gathered[r * 2 + half, h * 8 : h * 8 + 8, :] for r in range(8)], axis=0
            )
            turned = [tile] + [pltpu.roll(tile, k * 32, 1) for k in range(1, 4)]
            for d in range(4):
                for i in range(4):
                    spread[
                        h, d * 256 + i * 64 : d * 256 + i * 64 + 64, half * 128 : half * 128 + 128
                    ] = jnp.where(lane // 32 == i, turned[(i - d) % 4], 0.0).astype(BF16)


def grads_kernel(
    blocks, cot_hbm, w_scaled_ref, out_ref,
    cot_ref, gathered, spread, left_ref, left_t_ref, grad, left_sum, right_sum, arrived,
):
    copy = pltpu.make_async_copy(cot_hbm, cot_ref, arrived)
    copy.start()
    odd, seq = lax.axis_index("col") % 2, lax.axis_index("seq")
    low = lax.broadcasted_iota(jnp.int32, (32, LANES), 1) < 64
    fill(blocks, left_ref, gathered, spread)
    left_t_ref[...] = left_ref[...].astype(F32).T.astype(BF16)
    copy.wait()
    for i in range(16):
        cot = cot_ref[i * 4 : i * 4 + 4].reshape(256, LANES)
        for h in range(8):
            piece = dot(w_scaled_ref[h * 128 : h * 128 + 128, :], cot, (1, 1)).astype(BF16)
            for d in range(4):
                grad[h, i * 32 : i * 32 + 32, d * 256 : d * 256 + 256] = piece[d * 32 : d * 32 + 32]
    for h in range(8):
        part = dot(grad[h], spread[h], (1, 0))
        left_sum[...] = part if h == 0 else left_sum[...] + part
        for half in range(2):
            parts = []
            part = dot(left_t_ref[half * 128 : half * 128 + 128, :], grad[h], (1, 0))
            for d in range(4):
                lo = part[:, d * 256 : d * 256 + 128]
                hi = part[:, d * 256 + 128 : d * 256 + 256]
                parts.append(
                    jnp.where(low, lo[0:32], lo[32:64]) + jnp.where(low, hi[64:96], hi[96:128])
                )
            turned = jnp.concatenate(parts, axis=0).T
            total = turned[0:64] + turned[64:128]
            for r in range(8):
                right_sum[r * 2 + half, h * 8 : h * 8 + 8, :] = total[r * 8 : r * 8 + 8]
    none = jnp.zeros((LANES, LANES), BF16)
    for b in range(8):
        for half in range(2):
            out_ref[seq * 8 + b, half * 64 : half * 64 + 64] = left_sum[
                b * 64 : b * 64 + 64, half * 128 : half * 128 + 128
            ].astype(BF16)
            out_ref[odd * 8 + b, 128 + half * 64 : 192 + half * 64] = right_sum[
                b * 2 + half
            ].astype(BF16)
        out_ref[(1 - seq) * 8 + b, 0:128] = none
        out_ref[(1 - odd) * 8 + b, 128:256] = none


def pair_kernel(
    blocks, cot_ref, w_turned_ref, bias_ref, pair_ref, keep_out, send_out,
    gathered, spread, left_ref, outer, wout_sum, wout_rows,
):
    core = lax.axis_index("core")
    fill(blocks, left_ref, gathered, spread)
    left_ref[...] = (left_ref[...].astype(F32) * (1.0 / 64.0)).astype(BF16)
    for h in range(8):
        for d in range(4):
            piece = dot(left_ref[...], spread[h, d * 256 : d * 256 + 256, :], (1, 1)).astype(BF16)
            first = h * 128 + d * 32
            outer[:, first : first + 32, :] = piece.reshape(16, 32, 256)
    for i in range(16):
        cot = cot_ref[i * 4 : i * 4 + 4].reshape(256, LANES)
        tile = outer[i]
        turned = dot(w_turned_ref[...], tile, (1, 0))
        pair_ref[i * 4 : i * 4 + 4] = (
            (turned.T + bias_ref[...]).astype(BF16).reshape(4, 64, LANES)
        )
        part = dot(tile, cot, (1, 0))
        wout_sum[...] = part if i == 0 else wout_sum[...] + part
    for d in range(32):
        wout_rows[pl.ds(d, 32, stride=32), :] = wout_sum[d * 32 : d * 32 + 32, :]
    for z in range(4):
        for half in range(2):
            for out, owner in ((keep_out, core), (send_out, 1 - core)):
                b = (z * 2 + owner) * 2 + half
                out[z * 2 + half] = wout_rows[pl.ds(pl.multiple_of(b * 64, 64), 64), :].astype(BF16)


def sort_kernel(back_ref, keep_w, send_w, left_ref, other_ref, keep_ref, send_ref):
    core, upper, seq = lax.axis_index("core"), lax.axis_index("col") // 8, lax.axis_index("seq")
    for half, out in ((seq, left_ref), (1 - seq, other_ref)):
        rows = pl.ds(pl.multiple_of(half * 64, 64), 64)
        left = back_ref[0, rows].astype(F32)
        for b in range(1, 16):
            left += back_ref[b, rows].astype(F32)
        out[...] = left.astype(BF16)
    for z in range(4):
        for half in range(2):
            for out, owner, wout in ((keep_ref, core, keep_w), (send_ref, 1 - core, send_w)):
                c = (z * 2 + owner) * 2 + upper
                out[z * 2 + half, 0:64] = back_ref[c, 128 + half * 64 : 192 + half * 64]
                out[z * 2 + half, 64:128] = wout[z * 2 + half]


def turn_grads(left, right, rows_ref, turn_ref):
    rows_ref[...] = right
    rows = [rows_ref[pl.ds(j, 8, stride=8), :] for j in range(8)]
    for half in range(2):
        for k in range(4):
            turn_ref[half, pl.ds(k, 8, stride=4), :] = jnp.concatenate(
                [rows[half * 4 + j][:, k * 32 : k * 32 + 32] for j in range(4)], axis=1
            )
    right = jnp.concatenate([turn_ref[0], turn_ref[1]], axis=1).astype(BF16)
    left = jnp.concatenate([left[0:32], left[32:64]], axis=1).astype(BF16)
    return left, right


def weights_kernel(
    left_ref, partner_ref, right_ref, normed_ref, partner_normed, keep_ref, send_ref, rows_ref, turn_ref, total_ref
):
    core = lax.axis_index("core")
    left, right = turn_grads(
        left_ref[...].astype(F32), right_ref[...].astype(F32), rows_ref, turn_ref
    )
    partner = jnp.concatenate([partner_ref[0:32], partner_ref[32:64]], axis=1)
    left = dot(left, normed_ref[...], (1, 0)) + dot(partner, partner_normed[...], (1, 0))
    total = jnp.concatenate([left, dot(right, normed_ref[...], (1, 0))], axis=0)
    total_ref[0] = total[:, 0:128]
    total_ref[1] = total[:, 128:256]
    keep_ref[...] = total_ref[core]
    send_ref[...] = total_ref[1 - core].astype(BF16)


def align_kernel(x_ref, left_w, right_w, left_ref, right_ref, align_ref, rows_ref, block_ref, turn_ref):
    scaled, invstd = normalize(x_ref, rows_ref)
    left, right = turn_grads(
        left_ref[...].astype(F32), right_ref[...].astype(F32), block_ref, turn_ref
    )
    normed_grad = dot(left, left_w[...], (0, 0)) + dot(right, right_w[...], (0, 0))
    mean_grad = jnp.mean(normed_grad, axis=1, keepdims=True)
    mean_cross = jnp.mean(normed_grad * scaled, axis=1, keepdims=True)
    result = invstd * (normed_grad - mean_grad - scaled * mean_cross)
    for h in range(2):
        for i in range(8):
            rows_ref[h, pl.ds(i, SEQ_HALF, stride=8), :] = result[
                i * 32 : i * 32 + 32, h * 128 : h * 128 + 128
            ]
        align_ref[:, h * 128 : h * 128 + 128] = rows_ref[h]


def last_kernel(own_ref, other_ref, wout_ref, left_ref, right_ref):
    core = lax.axis_index("core")
    sums = []
    for blocks in (own_ref, other_ref):
        weight = blocks[0, 0:64].astype(F32)
        for b in range(1, 8):
            weight += blocks[b, 0:64].astype(F32)
        sums.append(weight * (1.0 / 1024.0))
    for half, weight in enumerate(
        (jnp.where(core == 0, sums[0], sums[1]), jnp.where(core == 0, sums[1], sums[0]))
    ):
        left_ref[:, half * 128 : half * 128 + 128] = weight[0:32]
        right_ref[:, half * 128 : half * 128 + 128] = weight[32:64]
    for z in range(4):
        for half in range(2):
            for blocks, owner in ((own_ref, core), (other_ref, 1 - core)):
                start = pl.multiple_of(((z * 2 + owner) * 2 + half) * 64, 64)
                wout_ref[pl.ds(start, 64), :] = blocks[z * 2 + half, 64:128].astype(F32) * (
                    1.0 / 1024.0
                )


def body(alignment, left_weight, right_weight, out_weight, out_bias, cotangent):
    cols_n, seq_n = lax.axis_size("col"), lax.axis_size("seq")
    column = ("z", "seq")
    to_partner = [(c * seq_n + c // 8, c * seq_n + 1 - c // 8) for c in range(cols_n)]
    struct = jax.ShapeDtypeStruct
    vmem = pltpu.VMEM
    left_w, right_w = left_weight.T, right_weight.T
    w_rows = out_weight.reshape(CP, CP, LANES).transpose(1, 0, 2).reshape(CP * CP, LANES)
    w_scaled = (w_rows.astype(F32) * (1.0 / 64.0)).astype(BF16)
    w_turned = w_rows.T
    col = lax.axis_index("col")
    seq = lax.axis_index("seq")
    def exchange(value, axes):
        return lax.all_to_all(value, axes, 0, 0, tiled=True)

    def gather(value, axes, count):
        return exchange(jnp.broadcast_to(value, (count,) + value.shape), axes)

    def total(value):
        return jnp.sum(value.astype(F32), axis=0).astype(BF16)

    def other_core(value):
        return lax.ppermute(value, "core", [(0, 1), (1, 0)])

    def cost(flops, nbytes):
        return pl.CostEstimate(flops=flops, bytes_accessed=nbytes, transcendentals=0)

    def in_hbm(value):
        return pltpu.with_memory_space_constraint(value, pltpu.HBM)

    block = struct((64, LANES), BF16)
    both, normed = pl.pallas_call(
        project_kernel,
        out_shape=(struct((8, 128, LANES), BF16), struct((256, 256), BF16)),
        scratch_shapes=[vmem((2, 256, LANES), F32), vmem((64, LANES), F32)],
        compiler_params=params(8),
        name="project",
    )(in_hbm(alignment), in_hbm(left_w), in_hbm(right_w))

    both = exchange(both, column)
    vm, hbm = pl.BlockSpec(memory_space=vmem), pl.BlockSpec(memory_space=pl.ANY)
    blocks = pl.pallas_call(
        route_kernel,
        in_specs=[vm, vm],
        out_shape=struct((16, 256, LANES), BF16),
        compiler_params=params(8),
        name="route",
    )(both, other_core(both))
    blocks = exchange(blocks, "col")
    partner_normed = lax.ppermute(normed, ("col", "seq"), [(b, a) for a, b in to_partner])
    blocks, partner_normed = lax.optimization_barrier((blocks, partner_normed))

    gathered, spread = vmem((16, 64, LANES), F32), vmem((8, 1024, 256), BF16)
    left_rows = vmem((512, 256), BF16)
    back = pl.pallas_call(
        grads_kernel,
        in_specs=[vm, hbm, vm],
        out_shape=struct((16, 256, LANES), BF16),
        scratch_shapes=[
            vmem((64, 64, LANES), BF16),
            gathered,
            spread,
            left_rows,
            vmem((256, 512), BF16),
            vmem((8, 512, 1024), BF16),
            vmem((512, 256), F32),
            vmem((16, 64, LANES), F32),
            pltpu.SemaphoreType.DMA,
        ],
        compiler_params=params(24),
        cost_estimate=cost(4 << 30, 4 << 20),
        name="grads",
    )(blocks, in_hbm(cotangent), w_scaled)
    back = exchange(back, "col")
    eight = struct((8, 64, LANES), BF16)
    pair, keep, send = pl.pallas_call(
        pair_kernel,
        in_specs=[vm] * 4,
        out_shape=(struct((64, 64, LANES), BF16), eight, eight),
        scratch_shapes=[
            gathered,
            spread,
            left_rows,
            vmem((16, 1024, 256), BF16),
            vmem((1024, LANES), F32),
            vmem((1024, LANES), F32),
        ],
        compiler_params=params(24),
        cost_estimate=cost(4 << 30, 4 << 20),
        name="pair_tile",
    )(blocks, in_hbm(cotangent), w_turned, out_bias.reshape(1, LANES))
    sixteen = struct((8, 128, LANES), BF16)
    left_grad, other_left, keep, send = pl.pallas_call(
        sort_kernel,
        in_specs=[vm] * 3,
        out_shape=(block, block, sixteen, sixteen),
        compiler_params=params(8),
        name="sort",
    )(back, keep, send)
    first = total(exchange((keep.astype(F32) + other_core(send).astype(F32)).astype(BF16), column))
    right_grad = first[:64]
    keep_w, send_w = pl.pallas_call(
        weights_kernel,
        out_shape=(struct((64, LANES), F32), block),
        scratch_shapes=[
            vmem((64, LANES), F32),
            vmem((2, 32, LANES), F32),
            vmem((2, 64, LANES), F32),
        ],
        compiler_params=params(8),
        name="weight_grads",
    )(left_grad, other_left, right_grad, normed, partner_normed)
    weight = (keep_w + other_core(send_w).astype(F32)).astype(BF16)
    stage = total(gather(jnp.concatenate([weight, first[64:]], axis=0), "col", 16))
    other_left = lax.ppermute(other_left, ("col", "seq"), to_partner)
    stage, other_left = lax.optimization_barrier((stage, other_left))
    last = gather(stage, column, 8)
    home = lax.axis_index("col") // 8 == lax.axis_index("seq")
    left_grad = jnp.where(home, left_grad, other_left)
    align_grad = pl.pallas_call(
        align_kernel,
        out_shape=struct((256, 256), F32),
        scratch_shapes=[vmem((2, 256, LANES), F32), vmem((64, LANES), F32), vmem((2, 32, LANES), F32)],
        compiler_params=params(8),
        cost_estimate=cost(1 << 24, 1 << 20),
        name="align",
    )(in_hbm(alignment), left_w, right_w, left_grad, right_grad)
    last, align_grad = lax.optimization_barrier((last, align_grad))
    wout_grad, left_weight_grad, right_weight_grad = pl.pallas_call(
        last_kernel,
        out_shape=(struct((1024, LANES), F32), struct((32, 256), F32), struct((32, 256), F32)),
        compiler_params=params(8),
        name="last",
    )(last, other_core(last))
    return (
        pair,
        align_grad.reshape(alignment.shape),
        left_weight_grad.T,
        right_weight_grad.T,
        wout_grad,
    )


def solution(mesh):
    z = mesh.shape["row"] // 2
    fine = Mesh(
        mesh.devices.reshape(z, 2, mesh.shape["col"], mesh.shape["seq"]), ("z", "core", "col", "seq")
    )
    row = ("z", "core")
    tiles, blocks = P(row + ("seq",), "col", None), P("seq", row + ("col",), None)
    return jax.shard_map(
        body,
        mesh=fine,
        in_specs=(blocks, P(), P(), P(), P(), tiles),
        out_specs=(tiles, blocks, P(), P(), P()),
        check_vma=False,
    )
```

time: 144 us -> 129 us (0.90)
  starting transfers between devices: 65.1 us -> 37.2 us
  blocking collectives: 13.6 us -> 27.4 us
  Pallas kernels: 18.9 us -> 23.4 us
  waiting for transfers between devices: 39.5 us -> 36.1 us
    all_to_all x6 -> x4, starting transfers between devices: 42.4 us -> 19.6 us  [exchange(): return lax.all_to_all(value, axes, 0, 0, tiled=True)]
    all_to_all x6 -> x4, waiting for transfers between devices: 36.9 us -> 23.1 us  [exchange(): return lax.all_to_all(value, axes, 0, 0, tiled=True)]
    all_to_all x1 -> x2, blocking collectives: 13.6 us -> 27.4 us  [exchange(): return lax.all_to_all(value, axes, 0, 0, tiled=True)]
    ppermute x4 -> x2, starting transfers between devices: 12.6 us -> 6.11 us  [the longest x1 4.82 us: body(): other_left = lax.ppermute(other_left, ('col', 'seq'), to_partner)]
    ppermute x4 -> x2, waiting for transfers between devices: 2.57 us -> 8.69 us  [the longest x1 8.69 us: body(): lax.ppermute(normed, ('col', 'seq'), [(b, a) for a, b in to_partner])]
    pallas_call x3 -> x6, Pallas kernels: 15.9 us -> 20.4 us  [the longest x1 9 us: body(): pl.pallas_call(grads_kernel, in_specs=[vm, hbm, vm], out_shape=struct((16...]
    ppermute x2 -> x4, waiting for transfers between devices: 0.01 us -> 4.33 us  [other_core(): return lax.ppermute(value, 'core', [(0, 1), (1, 0)])]
    ppermute x2 -> x4, starting transfers between devices: 10.1 us -> 11.5 us  [other_core(): return lax.ppermute(value, 'core', [(0, 1), (1, 0)])]
  transfers between devices with their start and end apart: 12 -> 10, of which waited for: 8 -> 9; matrix products, arithmetic and copies ran while one was open for 1% -> 0% of each run, Pallas kernels for 1% -> 8%
where the time goes in v3:
time: 129 us; the launch traced here: 128 us
  starting transfers between devices  37.2 us (29%)
  waiting for transfers between devices  36.1 us (28%)
  blocking collectives  27.4 us (21%)
  Pallas kernels  23.4 us (18%)
  local copies, waits for them, and re-layouts  3.25 us (3%)
    all_to_all x2, blocking collectives, exchange(): return lax.all_to_all(value, axes, 0, 0, tiled=True)  27.4 us
    all_to_all x4, waiting for transfers between devices, exchange(): return lax.all_to_all(value, axes, 0, 0, tiled=True)  23.1 us
    all_to_all x4, starting transfers between devices, exchange(): return lax.all_to_all(value, axes, 0, 0, tiled=True)  19.6 us
    ppermute x4, starting transfers between devices, other_core(): return lax.ppermute(value, 'core', [(0, 1), (1, 0)])  11.5 us
    pallas_call x1, Pallas kernels, body(): pl.pallas_call(grads_kernel, in_specs=[vm, hbm, vm], out_shape=struct((16...  9 us
    ppermute x1, waiting for transfers between devices, body(): lax.ppermute(normed, ('col', 'seq'), [(b, a) for a, b in to_partner])  8.69 us
    pallas_call x1, Pallas kernels, body(): pl.pallas_call(pair_kernel, in_specs=[vm] * 4, out_shape=(struct((64, 64,...  8.5 us
    ppermute x1, starting transfers between devices, body(): other_left = lax.ppermute(other_left, ('col', 'seq'), to_partner)  4.82 us
  transfers between devices with their start and end apart: 10, of which 9 were waited for; matrix products, arithmetic and copies ran while one was open for 0% of the time, Pallas kernels for 8%

profile of v3, /device:TPU:1, one launch (start us, length us, event | category | flops | bytes accessed | tf_op | source)
XLA Modules:
  0.0 128.4 jit_solution(3838498639313577952)
XLA Ops:
  0.6 1.4 %project.1 = (bf16[8,128,128]{2,1,0:T(8,128)(2,1)S(1)}, bf16[256,256]{1,0:T(8,128)(2,1)S(1)}) custom-call(bf16[32,8,256]{2,1,0:T(8,128)(2,1)} %x_ref.3, bf16[32,256]{1,0:T(8,128)(2,1)} %bitcast.13, bf16[32,256]{1,0:T(8,128)(2,1)} %bitcast.15), custom_call_target="tpu_custom_call" | custom-call | tf_op jit(solution)/shard_map/project/pallas_call | solution.py:290
  2.1 15.9 %all_to_all.30.own_ref = bf16[8,128,128]{2,1,0:T(8,128)(2,1)S(1)} all-to-all(bf16[8,128,128]{2,1,0:T(8,128)(2,1)S(1)} %get-tuple-element.25), channel_id=1, replica_groups=mesh['z'=4,'core'=2,'col'=16,'seq'=2] {'z','seq'}, dimensions={0} | all-to-all | bytes 524288 | tf_op jit(solution)/shard_map/all_to_all | solution.py:272
  18.0 2.7 %collective-permute-start = (bf16[8,128,128]{2,1,0:T(8,128)(2,1)S(1)}, bf16[8,128,128]{2,1,0:T(8,128)(2,1)S(1)}, u32[]{:S(2)}, u32[]{:S(2)}) collective-permute-start(bf16[8,128,128]{2,1,0:T(8,128)(2,1)S(1)} %all_to_all.30.own_ref), channel_id=1, source_target_pairs={{0,32},{32,0},{1,33},{33,1},{2,34},{34,2},{3,35},{35,3},{4,36},{36... | collective-permute-start | bytes 786440 | tf_op jit(solution)/shard_map/ppermute | solution.py:281
  20.7 1.2 collective-permute-done.other_ref
  21.9 1.1 route.1
  23.0 0.0 copy-start.3
  23.0 6.9 %all-to-all-start.1 = ((bf16[16,256,128]{2,1,0:T(8,128)(2,1)}), bf16[16,256,128]{2,1,0:T(8,128)(2,1)S(1)}, u32[]{:S(2)}, u32[]{:S(2)}) async-start(bf16[16,256,128]{2,1,0:T(8,128)(2,1)} %route.1), calls=%async_computation.1 | async-start | bytes 2097152 | tf_op jit(solution)/shard_map/all_to_all | solution.py:272
  29.9 1.3 %collective-permute-start.1 = (bf16[256,256]{1,0:T(8,128)(2,1)S(1)}, bf16[256,256]{1,0:T(8,128)(2,1)S(1)}, u32[]{:S(2)}, u32[]{:S(2)}) collective-permute-start(bf16[256,256]{1,0:T(8,128)(2,1)S(1)} %get-tuple-element.26.normed_ref), channel_id=1, source_target_pairs={{1,0},{3,2},{5,4},{7,6},{9,8},{11,10},{13,12},{15,14},{16,17},{18,... | collective-permute-start | bytes 393224 | tf_op jit(solution)/shard_map/ppermute | solution.py:308
  31.2 0.0 copy-done.3
  31.2 0.1 copy.13
  31.3 0.1 multiply_convert_fusion.w_scaled_ref
  31.4 8.7 %collective-permute-done.1.partner_normed = bf16[256,256]{1,0:T(8,128)(2,1)S(1)} collective-permute-done((bf16[256,256]{1,0:T(8,128)(2,1)S(1)}, bf16[256,256]{1,0:T(8,128)(2,1)S(1)}, u32[]{:S(2)}, u32[]{:S(2)}) %collective-permute-start.1) | collective-permute-done | bytes 131104 | tf_op jit(solution)/shard_map/ppermute | solution.py:308
  40.1 6.1 %all-to-all-done.1.blocks = bf16[16,256,128]{2,1,0:T(8,128)(2,1)S(1)} async-done(((bf16[16,256,128]{2,1,0:T(8,128)(2,1)}), bf16[16,256,128]{2,1,0:T(8,128)(2,1)S(1)}, u32[]{:S(2)}, u32[]{:S(2)}) %all-to-all-start.1) | async-done | bytes 1048608 | tf_op jit(solution)/shard_map/all_to_all | solution.py:272
  46.2 9.0 %grads.1 = bf16[16,256,128]{2,1,0:T(8,128)(2,1)} custom-call(bf16[16,256,128]{2,1,0:T(8,128)(2,1)S(1)} %all-to-all-done.1.blocks, bf16[64,64,128]{2,1,0:T(8,128)(2,1)} %cot_hbm.1, bf16[1024,128]{1,0:T(8,128)(2,1)S(1)} %multiply_convert_fusion.w_scaled_ref), custom_call_target="tpu_custom_call" | custom-call | flops 4294967296 | bytes 4194304 | tf_op jit(solution)/shard_map/grads/pallas_call | solution.py:313
  55.2 4.6 %all-to-all-start.2 = ((bf16[16,256,128]{2,1,0:T(8,128)(2,1)}), bf16[16,256,128]{2,1,0:T(8,128)(2,1)S(1)}, u32[]{:S(2)}, u32[]{:S(2)}) async-start(bf16[16,256,128]{2,1,0:T(8,128)(2,1)} %grads.1), calls=%async_computation.2 | async-start | bytes 2097152 | tf_op jit(solution)/shard_map/all_to_all | solution.py:272
  59.8 0.1 copy.14.w_turned_ref
  59.9 0.0 copy-start.2
  60.0 0.6 copy-done.2
  60.6 8.5 %pair_tile.1 = (bf16[64,64,128]{2,1,0:T(8,128)(2,1)}, bf16[8,64,128]{2,1,0:T(8,128)(2,1)S(1)}, bf16[8,64,128]{2,1,0:T(8,128)(2,1)S(1)}) custom-call(bf16[16,256,128]{2,1,0:T(8,128)(2,1)S(1)} %all-to-all-done.1.blocks, bf16[64,64,128]{2,1,0:T(8,128)(2,1)} %cot_hbm.1, bf16[128,1024]{1,0:T(8,128)(2,1)S(1)} %copy.14.w_turned_ref, f32[1,128]{1,0:T(1,128)S(1)} %bitcast.17), custom_call_target="tpu_custom_call" | custom-call | flops 4294967296 | bytes 4194304 | tf_op jit(solution)/shard_map/pair_tile/pallas_call | solution.py:334
  69.1 6.4 %all-to-all-done.2.back_ref = bf16[16,256,128]{2,1,0:T(8,128)(2,1)S(1)} async-done(((bf16[16,256,128]{2,1,0:T(8,128)(2,1)}), bf16[16,256,128]{2,1,0:T(8,128)(2,1)S(1)}, u32[]{:S(2)}, u32[]{:S(2)}) %all-to-all-start.2) | async-done | bytes 1048608 | tf_op jit(solution)/shard_map/all_to_all | solution.py:272
  75.5 0.1 sort.1
  75.6 2.9 %collective-permute-start.2 = (bf16[8,128,128]{2,1,0:T(8,128)(2,1)S(1)}, bf16[8,128,128]{2,1,0:T(8,128)(2,1)S(1)}, u32[]{:S(2)}, u32[]{:S(2)}) collective-permute-start(bf16[8,128,128]{2,1,0:T(8,128)(2,1)S(1)} %get-tuple-element.34), channel_id=1, source_target_pairs={{0,32},{32,0},{1,33},{33,1},{2,34},{34,2},{3,35},{35,3},{4,36},{36... | collective-permute-start | bytes 786440 | tf_op jit(solution)/shard_map/ppermute | solution.py:281
  78.5 1.2 collective-permute-done.2
  79.7 0.1 add_convert_fusion
  79.8 11.5 %all_to_all.31 = bf16[8,128,128]{2,1,0:T(8,128)(2,1)S(1)} all-to-all(bf16[8,128,128]{2,1,0:T(8,128)(2,1)S(1)} %add_convert_fusion), channel_id=1, replica_groups=mesh['z'=4,'core'=2,'col'=16,'seq'=2] {'z','seq'}, dimensions={0} | all-to-all | bytes 524288 | tf_op jit(solution)/shard_map/all_to_all | solution.py:272
  91.3 0.2 weight_grads.1
  91.6 2.8 %collective-permute-start.3 = (bf16[64,128]{1,0:T(8,128)(2,1)S(1)}, bf16[64,128]{1,0:T(8,128)(2,1)S(1)}, u32[]{:S(2)}, u32[]{:S(2)}) collective-permute-start(bf16[64,128]{1,0:T(8,128)(2,1)S(1)} %get-tuple-element.37), channel_id=1, source_target_pairs={{0,32},{32,0},{1,33},{33,1},{2,34},{34,2},{3,35},{35,3},{4,36},{36... | collective-permute-start | bytes 49160 | tf_op jit(solution)/shard_map/ppermute | solution.py:281
  94.4 0.8 collective-permute-done.3
  95.2 0.9 broadcast_in_dim.6
  96.1 3.6 %all-to-all-start.4 = ((bf16[16,128,128]{2,1,0:T(8,128)(2,1)}), bf16[16,128,128]{2,1,0:T(8,128)(2,1)S(1)}, u32[]{:S(2)}, u32[]{:S(2)}) async-start(bf16[16,128,128]{2,1,0:T(8,128)(2,1)} %broadcast_in_dim.6), calls=%async_computation.4 | async-start | bytes 1048576 | tf_op jit(solution)/shard_map/all_to_all | solution.py:272
  99.7 4.8 %collective-permute-start.4 = (bf16[64,128]{1,0:T(8,128)(2,1)S(1)}, bf16[64,128]{1,0:T(8,128)(2,1)S(1)}, u32[]{:S(2)}, u32[]{:S(2)}) collective-permute-start(bf16[64,128]{1,0:T(8,128)(2,1)S(1)} %get-tuple-element.32.partner_ref), channel_id=1, source_target_pairs={{0,1},{2,3},{4,5},{6,7},{8,9},{10,11},{12,13},{14,15},{17,16},{19,... | collective-permute-start | bytes 49160 | tf_op jit(solution)/shard_map/ppermute | solution.py:373
  104.5 6.2 %all-to-all-done.4 = bf16[16,128,128]{2,1,0:T(8,128)(2,1)S(1)} async-done(((bf16[16,128,128]{2,1,0:T(8,128)(2,1)}), bf16[16,128,128]{2,1,0:T(8,128)(2,1)S(1)}, u32[]{:S(2)}, u32[]{:S(2)}) %all-to-all-start.4) | async-done | bytes 524320 | tf_op jit(solution)/shard_map/all_to_all | solution.py:272
  110.7 0.1 reduce_sum.25
  110.8 0.0 collective-permute-done.4
  110.8 0.7 broadcast_in_dim.7
  111.5 4.5 %all-to-all-start.5 = ((bf16[8,128,128]{2,1,0:T(8,128)(2,1)}), bf16[8,128,128]{2,1,0:T(8,128)(2,1)S(1)}, u32[]{:S(2)}, u32[]{:S(2)}) async-start(bf16[8,128,128]{2,1,0:T(8,128)(2,1)} %broadcast_in_dim.7), calls=%async_computation.5 | async-start | bytes 524288 | tf_op jit(solution)/shard_map/all_to_all | solution.py:272
  116.1 0.0 copy-start
  116.1 0.0 copy-start.1
  116.1 0.7 copy-done
  116.8 0.0 copy-done.1
  116.8 2.1 %align.1 = f32[256,256]{1,0:T(8,128)} custom-call(bf16[32,8,256]{2,1,0:T(8,128)(2,1)} %x_ref.3, bf16[32,256]{1,0:T(8,128)(2,1)S(1)} %bitcast.14, bf16[32,256]{1,0:T(8,128)(2,1)S(1)} %bitcast.16, bf16[64,128]{1,0:T(8,128)(2,1)S(1)} %broadcast_select_fusion.left_ref, bf16[64,128]{1,0:T(8,128)(2,1)S(1)} %get-tuple-element.45.right_ref), custom_call_target="tpu_custom_call" | custom-call | flops 16777216 | bytes 1048576 | tf_op jit(solution)/shard_map/align/pallas_call | solution.py:378
  118.9 4.4 %all-to-all-done.5.own_ref = bf16[8,128,128]{2,1,0:T(8,128)(2,1)S(1)} async-done(((bf16[8,128,128]{2,1,0:T(8,128)(2,1)}), bf16[8,128,128]{2,1,0:T(8,128)(2,1)S(1)}, u32[]{:S(2)}, u32[]{:S(2)}) %all-to-all-start.5) | async-done | bytes 262176 | tf_op jit(solution)/shard_map/all_to_all | solution.py:272
  123.3 3.1 %collective-permute-start.5 = (bf16[8,128,128]{2,1,0:T(8,128)(2,1)S(1)}, bf16[8,128,128]{2,1,0:T(8,128)(2,1)S(1)}, u32[]{:S(2)}, u32[]{:S(2)}) collective-permute-start(bf16[8,128,128]{2,1,0:T(8,128)(2,1)S(1)} %all-to-all-done.5.own_ref), channel_id=1, source_target_pairs={{0,32},{32,0},{1,33},{33,1},{2,34},{34,2},{3,35},{35,3},{4,36},{36... | collective-permute-start | bytes 786440 | tf_op jit(solution)/shard_map/ppermute | solution.py:281
  126.4 1.2 collective-permute-done.5.other_ref
  127.5 0.9 last.1
  (5 shorter events, 0.1 us)
Async XLA Ops:
  18.0 3.8 %collective-permute-start = (bf16[8,128,128]{2,1,0:T(8,128)(2,1)S(1)}, bf16[8,128,128]{2,1,0:T(8,128)(2,1)S(1)}, u32[]{:S(2)}, u32[]{:S(2)}) collective-permute-start(bf16[8,128,128]{2,1,0:T(8,128)(2,1)S(1)} %all_to_all.30.own_ref), channel_id=1, source_target_pairs={{0,32},{32,0},{1,33},{33,1},{2,34},{34,2},{3,35},{35,3},{4,36},{36... | collective-permute-start | bytes 786440 | tf_op jit(solution)/shard_map/ppermute | solution.py:281
  23.0 8.2 %copy-start.3 = (bf16[1024,128]{1,0:T(8,128)(2,1)S(1)}, bf16[1024,128]{1,0:T(8,128)(2,1)}, u32[]{:S(2)}) copy-start(bf16[1024,128]{1,0:T(8,128)(2,1)} %param.9) | copy-start | bytes 786436
  23.0 23.2 %all-to-all-start.1 = ((bf16[16,256,128]{2,1,0:T(8,128)(2,1)}), bf16[16,256,128]{2,1,0:T(8,128)(2,1)S(1)}, u32[]{:S(2)}, u32[]{:S(2)}) async-start(bf16[16,256,128]{2,1,0:T(8,128)(2,1)} %route.1), calls=%async_computation.1 | async-start | bytes 2097152 | tf_op jit(solution)/shard_map/all_to_all | solution.py:272
  29.9 10.2 %collective-permute-start.1 = (bf16[256,256]{1,0:T(8,128)(2,1)S(1)}, bf16[256,256]{1,0:T(8,128)(2,1)S(1)}, u32[]{:S(2)}, u32[]{:S(2)}) collective-permute-start(bf16[256,256]{1,0:T(8,128)(2,1)S(1)} %get-tuple-element.26.normed_ref), channel_id=1, source_target_pairs={{1,0},{3,2},{5,4},{7,6},{9,8},{11,10},{13,12},{15,14},{16,17},{18,... | collective-permute-start | bytes 393224 | tf_op jit(solution)/shard_map/ppermute | solution.py:308
  55.2 20.3 %all-to-all-start.2 = ((bf16[16,256,128]{2,1,0:T(8,128)(2,1)}), bf16[16,256,128]{2,1,0:T(8,128)(2,1)S(1)}, u32[]{:S(2)}, u32[]{:S(2)}) async-start(bf16[16,256,128]{2,1,0:T(8,128)(2,1)} %grads.1), calls=%async_computation.2 | async-start | bytes 2097152 | tf_op jit(solution)/shard_map/all_to_all | solution.py:272
  59.9 0.7 copy-start.2
  75.6 4.1 %collective-permute-start.2 = (bf16[8,128,128]{2,1,0:T(8,128)(2,1)S(1)}, bf16[8,128,128]{2,1,0:T(8,128)(2,1)S(1)}, u32[]{:S(2)}, u32[]{:S(2)}) collective-permute-start(bf16[8,128,128]{2,1,0:T(8,128)(2,1)S(1)} %get-tuple-element.34), channel_id=1, source_target_pairs={{0,32},{32,0},{1,33},{33,1},{2,34},{34,2},{3,35},{35,3},{4,36},{36... | collective-permute-start | bytes 786440 | tf_op jit(solution)/shard_map/ppermute | solution.py:281
  91.6 3.6 %collective-permute-start.3 = (bf16[64,128]{1,0:T(8,128)(2,1)S(1)}, bf16[64,128]{1,0:T(8,128)(2,1)S(1)}, u32[]{:S(2)}, u32[]{:S(2)}) collective-permute-start(bf16[64,128]{1,0:T(8,128)(2,1)S(1)} %get-tuple-element.37), channel_id=1, source_target_pairs={{0,32},{32,0},{1,33},{33,1},{2,34},{34,2},{3,35},{35,3},{4,36},{36... | collective-permute-start | bytes 49160 | tf_op jit(solution)/shard_map/ppermute | solution.py:281
  96.1 14.6 %all-to-all-start.4 = ((bf16[16,128,128]{2,1,0:T(8,128)(2,1)}), bf16[16,128,128]{2,1,0:T(8,128)(2,1)S(1)}, u32[]{:S(2)}, u32[]{:S(2)}) async-start(bf16[16,128,128]{2,1,0:T(8,128)(2,1)} %broadcast_in_dim.6), calls=%async_computation.4 | async-start | bytes 1048576 | tf_op jit(solution)/shard_map/all_to_all | solution.py:272
  99.7 11.1 %collective-permute-start.4 = (bf16[64,128]{1,0:T(8,128)(2,1)S(1)}, bf16[64,128]{1,0:T(8,128)(2,1)S(1)}, u32[]{:S(2)}, u32[]{:S(2)}) collective-permute-start(bf16[64,128]{1,0:T(8,128)(2,1)S(1)} %get-tuple-element.32.partner_ref), channel_id=1, source_target_pairs={{0,1},{2,3},{4,5},{6,7},{8,9},{10,11},{12,13},{14,15},{17,16},{19,... | collective-permute-start | bytes 49160 | tf_op jit(solution)/shard_map/ppermute | solution.py:373
  111.5 11.8 %all-to-all-start.5 = ((bf16[8,128,128]{2,1,0:T(8,128)(2,1)}), bf16[8,128,128]{2,1,0:T(8,128)(2,1)S(1)}, u32[]{:S(2)}, u32[]{:S(2)}) async-start(bf16[8,128,128]{2,1,0:T(8,128)(2,1)} %broadcast_in_dim.7), calls=%async_computation.5 | async-start | bytes 524288 | tf_op jit(solution)/shard_map/all_to_all | solution.py:272
  116.1 0.7 copy-start
  116.1 0.7 copy-start.1
  123.3 4.3 %collective-permute-start.5 = (bf16[8,128,128]{2,1,0:T(8,128)(2,1)S(1)}, bf16[8,128,128]{2,1,0:T(8,128)(2,1)S(1)}, u32[]{:S(2)}, u32[]{:S(2)}) collective-permute-start(bf16[8,128,128]{2,1,0:T(8,128)(2,1)S(1)} %all-to-all-done.5.own_ref), channel_id=1, source_target_pairs={{0,32},{32,0},{1,33},{33,1},{2,34},{34,2},{3,35},{35,3},{4,36},{36... | collective-permute-start | bytes 786440 | tf_op jit(solution)/shard_map/ppermute | solution.py:281

commit v4 on v3

--- a/solution.py
+++ b/solution.py
@@ -102,7 +102,7 @@
 ):
     copy = pltpu.make_async_copy(cot_hbm, cot_ref, arrived)
     copy.start()
-    odd, seq = lax.axis_index("col") % 2, lax.axis_index("seq")
+    odd = lax.axis_index("col") % 2
     low = lax.broadcasted_iota(jnp.int32, (32, LANES), 1) < 64
     fill(blocks, left_ref, gathered, spread)
     left_t_ref[...] = left_ref[...].astype(F32).T.astype(BF16)
@@ -132,14 +132,11 @@
     none = jnp.zeros((LANES, LANES), BF16)
     for b in range(8):
         for half in range(2):
-            out_ref[seq * 8 + b, half * 64 : half * 64 + 64] = left_sum[
+            out_ref[half * 8 + b, 0:64] = left_sum[
                 b * 64 : b * 64 + 64, half * 128 : half * 128 + 128
             ].astype(BF16)
-            out_ref[odd * 8 + b, 128 + half * 64 : 192 + half * 64] = right_sum[
-                b * 2 + half
-            ].astype(BF16)
-        out_ref[(1 - seq) * 8 + b, 0:128] = none
-        out_ref[(1 - odd) * 8 + b, 128:256] = none
+            out_ref[odd * 8 + b, 64 + half * 64 : 128 + half * 64] = right_sum[b * 2 + half].astype(BF16)
+        out_ref[(1 - odd) * 8 + b, 64:192] = none
 
 
 def pair_kernel(
@@ -172,19 +169,17 @@
                 out[z * 2 + half] = wout_rows[pl.ds(pl.multiple_of(b * 64, 64), 64), :].astype(BF16)
 
 
-def sort_kernel(back_ref, keep_w, send_w, left_ref, other_ref, keep_ref, send_ref):
-    core, upper, seq = lax.axis_index("core"), lax.axis_index("col") // 8, lax.axis_index("seq")
-    for half, out in ((seq, left_ref), (1 - seq, other_ref)):
-        rows = pl.ds(pl.multiple_of(half * 64, 64), 64)
-        left = back_ref[0, rows].astype(F32)
-        for b in range(1, 16):
-            left += back_ref[b, rows].astype(F32)
-        out[...] = left.astype(BF16)
+def sort_kernel(back_ref, keep_w, send_w, left_ref, keep_ref, send_ref):
+    core, upper = lax.axis_index("core"), lax.axis_index("col") // 8
+    left = back_ref[0, 0:64].astype(F32)
+    for b in range(1, 16):
+        left += back_ref[b, 0:64].astype(F32)
+    left_ref[...] = left.astype(BF16)
     for z in range(4):
         for half in range(2):
             for out, owner, wout in ((keep_ref, core, keep_w), (send_ref, 1 - core, send_w)):
                 c = (z * 2 + owner) * 2 + upper
-                out[z * 2 + half, 0:64] = back_ref[c, 128 + half * 64 : 192 + half * 64]
+                out[z * 2 + half, 0:64] = back_ref[c, 64 + half * 64 : 128 + half * 64]
                 out[z * 2 + half, 64:128] = wout[z * 2 + half]
 
 
@@ -202,15 +197,18 @@
 
 
 def weights_kernel(
-    left_ref, partner_ref, right_ref, normed_ref, partner_normed, keep_ref, send_ref, rows_ref, turn_ref, total_ref
+    left_ref, right_ref, far_normed, normed_ref, keep_ref, send_ref, rows_ref, turn_ref, total_ref
 ):
     core = lax.axis_index("core")
     left, right = turn_grads(
         left_ref[...].astype(F32), right_ref[...].astype(F32), rows_ref, turn_ref
     )
-    partner = jnp.concatenate([partner_ref[0:32], partner_ref[32:64]], axis=1)
-    left = dot(left, normed_ref[...], (1, 0)) + dot(partner, partner_normed[...], (1, 0))
-    total = jnp.concatenate([left, dot(right, normed_ref[...], (1, 0))], axis=0)
+    normed = normed_ref[...]
+    home = lax.axis_index("col") // 8 == lax.axis_index("seq")
+    left_normed = jnp.where(home, normed.astype(F32), far_normed[...].astype(F32)).astype(BF16)
+    total = jnp.concatenate(
+        [dot(left, left_normed, (1, 0)), dot(right, normed, (1, 0))], axis=0
+    )
     total_ref[0] = total[:, 0:128]
     total_ref[1] = total[:, 128:256]
     keep_ref[...] = total_ref[core]
@@ -259,7 +257,11 @@
 def body(alignment, left_weight, right_weight, out_weight, out_bias, cotangent):
     cols_n, seq_n = lax.axis_size("col"), lax.axis_size("seq")
     column = ("z", "seq")
-    to_partner = [(c * seq_n + c // 8, c * seq_n + 1 - c // 8) for c in range(cols_n)]
+    swap = [
+        (c * seq_n + s, c * seq_n + s if c // 8 == s else (c ^ 8) * seq_n + 1 - s)
+        for c in range(cols_n)
+        for s in range(seq_n)
+    ]
     struct = jax.ShapeDtypeStruct
     vmem = pltpu.VMEM
     left_w, right_w = left_weight.T, right_weight.T
@@ -305,15 +307,17 @@
         name="route",
     )(both, other_core(both))
     blocks = exchange(blocks, "col")
-    partner_normed = lax.ppermute(normed, ("col", "seq"), [(b, a) for a, b in to_partner])
-    blocks, partner_normed = lax.optimization_barrier((blocks, partner_normed))
+    to_home = [(c * seq_n + 1 - c // 8, c * seq_n + c // 8) for c in range(cols_n)]
+    across = [(c * seq_n + c // 8, (c ^ 8) * seq_n + c // 8) for c in range(cols_n)]
+    far_normed = lax.ppermute(normed, ("col", "seq"), to_home)
+    blocks, far_normed = lax.optimization_barrier((blocks, far_normed))
 
     gathered, spread = vmem((16, 64, LANES), F32), vmem((8, 1024, 256), BF16)
     left_rows = vmem((512, 256), BF16)
     back = pl.pallas_call(
         grads_kernel,
         in_specs=[vm, hbm, vm],
-        out_shape=struct((16, 256, LANES), BF16),
+        out_shape=struct((16, 192, LANES), BF16),
         scratch_shapes=[
             vmem((64, 64, LANES), BF16),
             gathered,
@@ -329,7 +333,9 @@
         cost_estimate=cost(4 << 30, 4 << 20),
         name="grads",
     )(blocks, in_hbm(cotangent), w_scaled)
-    back = exchange(back, "col")
+    far_normed, back = lax.optimization_barrier((far_normed, back))
+    far_normed = lax.ppermute(far_normed, ("col", "seq"), across)
+    back, far_normed = lax.optimization_barrier((exchange(back, "col"), far_normed))
     eight = struct((8, 64, LANES), BF16)
     pair, keep, send = pl.pallas_call(
         pair_kernel,
@@ -348,10 +354,10 @@
         name="pair_tile",
     )(blocks, in_hbm(cotangent), w_turned, out_bias.reshape(1, LANES))
     sixteen = struct((8, 128, LANES), BF16)
-    left_grad, other_left, keep, send = pl.pallas_call(
+    left_grad, keep, send = pl.pallas_call(
         sort_kernel,
         in_specs=[vm] * 3,
-        out_shape=(block, block, sixteen, sixteen),
+        out_shape=(block, sixteen, sixteen),
         compiler_params=params(8),
         name="sort",
     )(back, keep, send)
@@ -367,14 +373,12 @@
         ],
         compiler_params=params(8),
         name="weight_grads",
-    )(left_grad, other_left, right_grad, normed, partner_normed)
+    )(left_grad, right_grad, far_normed, normed)
     weight = (keep_w + other_core(send_w).astype(F32)).astype(BF16)
     stage = total(gather(jnp.concatenate([weight, first[64:]], axis=0), "col", 16))
-    other_left = lax.ppermute(other_left, ("col", "seq"), to_partner)
-    stage, other_left = lax.optimization_barrier((stage, other_left))
+    left_grad = lax.ppermute(left_grad, ("col", "seq"), swap)
+    stage, left_grad = lax.optimization_barrier((stage, left_grad))
     last = gather(stage, column, 8)
-    home = lax.axis_index("col") // 8 == lax.axis_index("seq")
-    left_grad = jnp.where(home, left_grad, other_left)
     align_grad = pl.pallas_call(
         align_kernel,
         out_shape=struct((256, 256), F32),

time: 129 us -> 128 us (level)
  waiting for transfers between devices: 36.1 us -> 34.3 us
  local copies, waits for them, and re-layouts: 3.25 us -> 1.91 us
    all_to_all x4, waiting for transfers between devices: 23.1 us -> 21.2 us  [exchange(): return lax.all_to_all(value, axes, 0, 0, tiled=True)]
    unnamed x8, local copies, waits for them, and re-layouts: 1.36 us -> 0.02 us
    ppermute x2 -> x3, starting transfers between devices: 6.11 us -> 6.92 us  [the longest x1 4.96 us: body(): far_normed = lax.ppermute(far_normed, ('col', 'seq'), across)]
    ppermute x2 -> x3, waiting for transfers between devices: 8.69 us -> 8.69 us  [the longest x1 8.69 us: body(): far_normed = lax.ppermute(normed, ('col', 'seq'), to_home)]
  transfers between devices with their start and end apart: 10 -> 11, of which waited for: 9 -> 8; matrix products, arithmetic and copies ran while one was open for 0% -> 0% of each run, Pallas kernels for 8% -> 8%
where the time goes in v4:
time: 128 us; the launch traced here: 127 us
  starting transfers between devices  37.9 us (30%)
  waiting for transfers between devices  34.3 us (27%)
  blocking collectives  28.6 us (22%)
  Pallas kernels  23.2 us (18%)
  local copies, waits for them, and re-layouts  1.91 us (1%)
    all_to_all x2, blocking collectives, exchange(): return lax.all_to_all(value, axes, 0, 0, tiled=True)  28.6 us
    all_to_all x4, waiting for transfers between devices, exchange(): return lax.all_to_all(value, axes, 0, 0, tiled=True)  21.2 us
    all_to_all x4, starting transfers between devices, exchange(): return lax.all_to_all(value, axes, 0, 0, tiled=True)  20.7 us
    ppermute x4, starting transfers between devices, other_core(): return lax.ppermute(value, 'core', [(0, 1), (1, 0)])  10.3 us
    pallas_call x1, Pallas kernels, body(): pl.pallas_call(grads_kernel, in_specs=[vm, hbm, vm], out_shape=struct((16...  8.91 us
    ppermute x1, waiting for transfers between devices, body(): far_normed = lax.ppermute(normed, ('col', 'seq'), to_home)  8.69 us
    pallas_call x1, Pallas kernels, body(): pl.pallas_call(pair_kernel, in_specs=[vm] * 4, out_shape=(struct((64, 64,...  8.51 us
    ppermute x1, starting transfers between devices, body(): far_normed = lax.ppermute(far_normed, ('col', 'seq'), across)  4.96 us
  transfers between devices with their start and end apart: 11, of which 8 were waited for; matrix products, arithmetic and copies ran while one was open for 0% of the time, Pallas kernels for 8%

profile of v4, /device:TPU:1, one launch (start us, length us, event | category | flops | bytes accessed | tf_op | source)
XLA Modules:
  0.0 127.0 jit_solution(3651726281916990833)
XLA Ops:
  0.6 1.4 %project.1 = (bf16[8,128,128]{2,1,0:T(8,128)(2,1)S(1)}, bf16[256,256]{1,0:T(8,128)(2,1)S(1)}) custom-call(bf16[32,8,256]{2,1,0:T(8,128)(2,1)} %x_ref.3, bf16[32,256]{1,0:T(8,128)(2,1)} %bitcast.13, bf16[32,256]{1,0:T(8,128)(2,1)} %bitcast.15), custom_call_target="tpu_custom_call" | custom-call | tf_op jit(solution)/shard_map/project/pallas_call | solution.py:292
  2.1 15.9 %all_to_all.30.own_ref = bf16[8,128,128]{2,1,0:T(8,128)(2,1)S(1)} all-to-all(bf16[8,128,128]{2,1,0:T(8,128)(2,1)S(1)} %get-tuple-element.28), channel_id=1, replica_groups=mesh['z'=4,'core'=2,'col'=16,'seq'=2] {'z','seq'}, dimensions={0} | all-to-all | bytes 524288 | tf_op jit(solution)/shard_map/all_to_all | solution.py:274
  18.0 2.7 %collective-permute-start = (bf16[8,128,128]{2,1,0:T(8,128)(2,1)S(1)}, bf16[8,128,128]{2,1,0:T(8,128)(2,1)S(1)}, u32[]{:S(2)}, u32[]{:S(2)}) collective-permute-start(bf16[8,128,128]{2,1,0:T(8,128)(2,1)S(1)} %all_to_all.30.own_ref), channel_id=1, source_target_pairs={{0,32},{32,0},{1,33},{33,1},{2,34},{34,2},{3,35},{35,3},{4,36},{36... | collective-permute-start | bytes 786440 | tf_op jit(solution)/shard_map/ppermute | solution.py:283
  20.7 1.2 collective-permute-done.other_ref
  21.9 1.1 route.1
  23.0 0.0 copy-start.3
  23.0 6.9 %all-to-all-start.1 = ((bf16[16,256,128]{2,1,0:T(8,128)(2,1)}), bf16[16,256,128]{2,1,0:T(8,128)(2,1)S(1)}, u32[]{:S(2)}, u32[]{:S(2)}) async-start(bf16[16,256,128]{2,1,0:T(8,128)(2,1)} %route.1), calls=%async_computation.1 | async-start | bytes 2097152 | tf_op jit(solution)/shard_map/all_to_all | solution.py:274
  29.9 1.3 %collective-permute-start.1 = (bf16[256,256]{1,0:T(8,128)(2,1)S(1)}, bf16[256,256]{1,0:T(8,128)(2,1)S(1)}, u32[]{:S(2)}, u32[]{:S(2)}) collective-permute-start(bf16[256,256]{1,0:T(8,128)(2,1)S(1)} %get-tuple-element.29.normed_ref), channel_id=1, source_target_pairs={{1,0},{3,2},{5,4},{7,6},{9,8},{11,10},{13,12},{15,14},{16,17},{18,... | collective-permute-start | bytes 393224 | tf_op jit(solution)/shard_map/ppermute | solution.py:312
  31.2 0.0 copy-done.3
  31.2 0.1 copy.13
  31.3 0.1 multiply_convert_fusion.w_scaled_ref
  31.4 8.7 %collective-permute-done.1 = bf16[256,256]{1,0:T(8,128)(2,1)S(1)} collective-permute-done((bf16[256,256]{1,0:T(8,128)(2,1)S(1)}, bf16[256,256]{1,0:T(8,128)(2,1)S(1)}, u32[]{:S(2)}, u32[]{:S(2)}) %collective-permute-start.1) | collective-permute-done | bytes 131104 | tf_op jit(solution)/shard_map/ppermute | solution.py:312
  40.1 6.1 %all-to-all-done.1.blocks = bf16[16,256,128]{2,1,0:T(8,128)(2,1)S(1)} async-done(((bf16[16,256,128]{2,1,0:T(8,128)(2,1)}), bf16[16,256,128]{2,1,0:T(8,128)(2,1)S(1)}, u32[]{:S(2)}, u32[]{:S(2)}) %all-to-all-start.1) | async-done | bytes 1048608 | tf_op jit(solution)/shard_map/all_to_all | solution.py:274
  46.2 8.9 %grads.1 = bf16[16,192,128]{2,1,0:T(8,128)(2,1)} custom-call(bf16[16,256,128]{2,1,0:T(8,128)(2,1)S(1)} %all-to-all-done.1.blocks, bf16[64,64,128]{2,1,0:T(8,128)(2,1)} %cot_hbm.1, bf16[1024,128]{1,0:T(8,128)(2,1)S(1)} %multiply_convert_fusion.w_scaled_ref), custom_call_target="tpu_custom_call" | custom-call | flops 4294967296 | bytes 4194304 | tf_op jit(solution)/shard_map/grads/pallas_call | solution.py:317
  55.1 4.5 %all-to-all-start.2 = ((bf16[16,192,128]{2,1,0:T(8,128)(2,1)}), bf16[16,192,128]{2,1,0:T(8,128)(2,1)S(1)}, u32[]{:S(2)}, u32[]{:S(2)}) async-start(bf16[16,192,128]{2,1,0:T(8,128)(2,1)} %grads.1), calls=%async_computation.2 | async-start | bytes 1572864 | tf_op jit(solution)/shard_map/all_to_all | solution.py:274
  59.7 0.1 copy.14.w_turned_ref
  59.8 0.0 copy-start.2
  59.9 5.0 %collective-permute-start.2 = (bf16[256,256]{1,0:T(8,128)(2,1)S(1)}, bf16[256,256]{1,0:T(8,128)(2,1)S(1)}, u32[]{:S(2)}, u32[]{:S(2)}) collective-permute-start(bf16[256,256]{1,0:T(8,128)(2,1)S(1)} %collective-permute-done.1), channel_id=1, source_target_pairs={{0,16},{2,18},{4,20},{6,22},{8,24},{10,26},{12,28},{14,30},{17,1},... | collective-permute-start | bytes 393224 | tf_op jit(solution)/shard_map/ppermute | solution.py:337
  64.8 0.0 copy-done.2
  64.8 8.5 %pair_tile.1 = (bf16[64,64,128]{2,1,0:T(8,128)(2,1)}, bf16[8,64,128]{2,1,0:T(8,128)(2,1)S(1)}, bf16[8,64,128]{2,1,0:T(8,128)(2,1)S(1)}) custom-call(bf16[16,256,128]{2,1,0:T(8,128)(2,1)S(1)} %all-to-all-done.1.blocks, bf16[64,64,128]{2,1,0:T(8,128)(2,1)} %cot_hbm.1, bf16[128,1024]{1,0:T(8,128)(2,1)S(1)} %copy.14.w_turned_ref, f32[1,128]{1,0:T(1,128)S(1)} %bitcast.17), custom_call_target="tpu_custom_call" | custom-call | flops 4294967296 | bytes 4194304 | tf_op jit(solution)/shard_map/pair_tile/pallas_call | solution.py:340
  73.3 0.0 collective-permute-done.2.far_normed
  73.4 0.0 all-to-all-done.2.back_ref
  73.4 0.1 sort.1
  73.4 1.8 %collective-permute-start.3 = (bf16[8,128,128]{2,1,0:T(8,128)(2,1)S(1)}, bf16[8,128,128]{2,1,0:T(8,128)(2,1)S(1)}, u32[]{:S(2)}, u32[]{:S(2)}) collective-permute-start(bf16[8,128,128]{2,1,0:T(8,128)(2,1)S(1)} %get-tuple-element.40), channel_id=1, source_target_pairs={{0,32},{32,0},{1,33},{33,1},{2,34},{34,2},{3,35},{35,3},{4,36},{36... | collective-permute-start | bytes 786440 | tf_op jit(solution)/shard_map/ppermute | solution.py:283
  75.2 1.2 collective-permute-done.3
  76.4 0.1 add_convert_fusion
  76.4 12.7 %all_to_all.31 = bf16[8,128,128]{2,1,0:T(8,128)(2,1)S(1)} all-to-all(bf16[8,128,128]{2,1,0:T(8,128)(2,1)S(1)} %add_convert_fusion), channel_id=1, replica_groups=mesh['z'=4,'core'=2,'col'=16,'seq'=2] {'z','seq'}, dimensions={0} | all-to-all | bytes 524288 | tf_op jit(solution)/shard_map/all_to_all | solution.py:274
  89.2 0.2 weight_grads.1
  89.4 2.8 %collective-permute-start.4 = (bf16[64,128]{1,0:T(8,128)(2,1)S(1)}, bf16[64,128]{1,0:T(8,128)(2,1)S(1)}, u32[]{:S(2)}, u32[]{:S(2)}) collective-permute-start(bf16[64,128]{1,0:T(8,128)(2,1)S(1)} %get-tuple-element.43), channel_id=1, source_target_pairs={{0,32},{32,0},{1,33},{33,1},{2,34},{34,2},{3,35},{35,3},{4,36},{36... | collective-permute-start | bytes 49160 | tf_op jit(solution)/shard_map/ppermute | solution.py:283
  92.2 0.8 collective-permute-done.4
  93.1 0.9 broadcast_in_dim.6
  94.0 4.3 %all-to-all-start.4 = ((bf16[16,128,128]{2,1,0:T(8,128)(2,1)}), bf16[16,128,128]{2,1,0:T(8,128)(2,1)S(1)}, u32[]{:S(2)}, u32[]{:S(2)}) async-start(bf16[16,128,128]{2,1,0:T(8,128)(2,1)} %broadcast_in_dim.6), calls=%async_computation.4 | async-start | bytes 1048576 | tf_op jit(solution)/shard_map/all_to_all | solution.py:274
  98.2 0.7 collective-permute-start.5
  98.9 10.1 %all-to-all-done.4 = bf16[16,128,128]{2,1,0:T(8,128)(2,1)S(1)} async-done(((bf16[16,128,128]{2,1,0:T(8,128)(2,1)}), bf16[16,128,128]{2,1,0:T(8,128)(2,1)S(1)}, u32[]{:S(2)}, u32[]{:S(2)}) %all-to-all-start.4) | async-done | bytes 524320 | tf_op jit(solution)/shard_map/all_to_all | solution.py:274
  109.0 0.1 reduce_sum.25
  109.1 0.0 collective-permute-done.5.left_ref
  109.1 0.7 broadcast_in_dim.7
  109.8 0.0 copy-start
  109.8 0.0 copy-start.1
  109.8 5.0 %all-to-all-start.5 = ((bf16[8,128,128]{2,1,0:T(8,128)(2,1)}), bf16[8,128,128]{2,1,0:T(8,128)(2,1)S(1)}, u32[]{:S(2)}, u32[]{:S(2)}) async-start(bf16[8,128,128]{2,1,0:T(8,128)(2,1)} %broadcast_in_dim.7), calls=%async_computation.5 | async-start | bytes 524288 | tf_op jit(solution)/shard_map/all_to_all | solution.py:274
  114.8 0.0 copy-done
  114.8 0.0 copy-done.1
  114.8 2.1 %align.1 = f32[256,256]{1,0:T(8,128)} custom-call(bf16[32,8,256]{2,1,0:T(8,128)(2,1)} %x_ref.3, bf16[32,256]{1,0:T(8,128)(2,1)S(1)} %bitcast.14, bf16[32,256]{1,0:T(8,128)(2,1)S(1)} %bitcast.16, bf16[64,128]{1,0:T(8,128)(2,1)S(1)} %collective-permute-done.5.left_ref, bf16[64,128]{1,0:T(8,128)(2,1)S(1)} %get-tuple-element.51.right_ref), custom_call_target="tpu_custom_call" | custom-call | flops 16777216 | bytes 1048576 | tf_op jit(solution)/shard_map/align/pallas_call | solution.py:382
  116.9 5.0 %all-to-all-done.5.own_ref = bf16[8,128,128]{2,1,0:T(8,128)(2,1)S(1)} async-done(((bf16[8,128,128]{2,1,0:T(8,128)(2,1)}), bf16[8,128,128]{2,1,0:T(8,128)(2,1)S(1)}, u32[]{:S(2)}, u32[]{:S(2)}) %all-to-all-start.5) | async-done | bytes 262176 | tf_op jit(solution)/shard_map/all_to_all | solution.py:274
  121.9 3.0 %collective-permute-start.6 = (bf16[8,128,128]{2,1,0:T(8,128)(2,1)S(1)}, bf16[8,128,128]{2,1,0:T(8,128)(2,1)S(1)}, u32[]{:S(2)}, u32[]{:S(2)}) collective-permute-start(bf16[8,128,128]{2,1,0:T(8,128)(2,1)S(1)} %all-to-all-done.5.own_ref), channel_id=1, source_target_pairs={{0,32},{32,0},{1,33},{33,1},{2,34},{34,2},{3,35},{35,3},{4,36},{36... | collective-permute-start | bytes 786440 | tf_op jit(solution)/shard_map/ppermute | solution.py:283
  124.9 1.2 collective-permute-done.6.other_ref
  126.1 0.9 last.1
  (4 shorter events, 0.1 us)
Async XLA Ops:
  18.0 3.8 %collective-permute-start = (bf16[8,128,128]{2,1,0:T(8,128)(2,1)S(1)}, bf16[8,128,128]{2,1,0:T(8,128)(2,1)S(1)}, u32[]{:S(2)}, u32[]{:S(2)}) collective-permute-start(bf16[8,128,128]{2,1,0:T(8,128)(2,1)S(1)} %all_to_all.30.own_ref), channel_id=1, source_target_pairs={{0,32},{32,0},{1,33},{33,1},{2,34},{34,2},{3,35},{35,3},{4,36},{36... | collective-permute-start | bytes 786440 | tf_op jit(solution)/shard_map/ppermute | solution.py:283
  23.0 8.2 %copy-start.3 = (bf16[1024,128]{1,0:T(8,128)(2,1)S(1)}, bf16[1024,128]{1,0:T(8,128)(2,1)}, u32[]{:S(2)}) copy-start(bf16[1024,128]{1,0:T(8,128)(2,1)} %param.9) | copy-start | bytes 786436
  23.0 23.2 %all-to-all-start.1 = ((bf16[16,256,128]{2,1,0:T(8,128)(2,1)}), bf16[16,256,128]{2,1,0:T(8,128)(2,1)S(1)}, u32[]{:S(2)}, u32[]{:S(2)}) async-start(bf16[16,256,128]{2,1,0:T(8,128)(2,1)} %route.1), calls=%async_computation.1 | async-start | bytes 2097152 | tf_op jit(solution)/shard_map/all_to_all | solution.py:274
  29.9 10.2 %collective-permute-start.1 = (bf16[256,256]{1,0:T(8,128)(2,1)S(1)}, bf16[256,256]{1,0:T(8,128)(2,1)S(1)}, u32[]{:S(2)}, u32[]{:S(2)}) collective-permute-start(bf16[256,256]{1,0:T(8,128)(2,1)S(1)} %get-tuple-element.29.normed_ref), channel_id=1, source_target_pairs={{1,0},{3,2},{5,4},{7,6},{9,8},{11,10},{13,12},{15,14},{16,17},{18,... | collective-permute-start | bytes 393224 | tf_op jit(solution)/shard_map/ppermute | solution.py:312
  55.1 18.2 %all-to-all-start.2 = ((bf16[16,192,128]{2,1,0:T(8,128)(2,1)}), bf16[16,192,128]{2,1,0:T(8,128)(2,1)S(1)}, u32[]{:S(2)}, u32[]{:S(2)}) async-start(bf16[16,192,128]{2,1,0:T(8,128)(2,1)} %grads.1), calls=%async_computation.2 | async-start | bytes 1572864 | tf_op jit(solution)/shard_map/all_to_all | solution.py:274
  59.8 5.0 %copy-start.2 = (f32[128]{0:T(128)S(1)}, f32[128]{0:T(128)}, u32[]{:S(2)}) copy-start(f32[128]{0:T(128)} %param.10) | copy-start | bytes 1540
  59.9 13.5 %collective-permute-start.2 = (bf16[256,256]{1,0:T(8,128)(2,1)S(1)}, bf16[256,256]{1,0:T(8,128)(2,1)S(1)}, u32[]{:S(2)}, u32[]{:S(2)}) collective-permute-start(bf16[256,256]{1,0:T(8,128)(2,1)S(1)} %collective-permute-done.1), channel_id=1, source_target_pairs={{0,16},{2,18},{4,20},{6,22},{8,24},{10,26},{12,28},{14,30},{17,1},... | collective-permute-start | bytes 393224 | tf_op jit(solution)/shard_map/ppermute | solution.py:337
  73.4 3.0 %collective-permute-start.3 = (bf16[8,128,128]{2,1,0:T(8,128)(2,1)S(1)}, bf16[8,128,128]{2,1,0:T(8,128)(2,1)S(1)}, u32[]{:S(2)}, u32[]{:S(2)}) collective-permute-start(bf16[8,128,128]{2,1,0:T(8,128)(2,1)S(1)} %get-tuple-element.40), channel_id=1, source_target_pairs={{0,32},{32,0},{1,33},{33,1},{2,34},{34,2},{3,35},{35,3},{4,36},{36... | collective-permute-start | bytes 786440 | tf_op jit(solution)/shard_map/ppermute | solution.py:283
  89.4 3.6 %collective-permute-start.4 = (bf16[64,128]{1,0:T(8,128)(2,1)S(1)}, bf16[64,128]{1,0:T(8,128)(2,1)S(1)}, u32[]{:S(2)}, u32[]{:S(2)}) collective-permute-start(bf16[64,128]{1,0:T(8,128)(2,1)S(1)} %get-tuple-element.43), channel_id=1, source_target_pairs={{0,32},{32,0},{1,33},{33,1},{2,34},{34,2},{3,35},{35,3},{4,36},{36... | collective-permute-start | bytes 49160 | tf_op jit(solution)/shard_map/ppermute | solution.py:283
  94.0 15.0 %all-to-all-start.4 = ((bf16[16,128,128]{2,1,0:T(8,128)(2,1)}), bf16[16,128,128]{2,1,0:T(8,128)(2,1)S(1)}, u32[]{:S(2)}, u32[]{:S(2)}) async-start(bf16[16,128,128]{2,1,0:T(8,128)(2,1)} %broadcast_in_dim.6), calls=%async_computation.4 | async-start | bytes 1048576 | tf_op jit(solution)/shard_map/all_to_all | solution.py:274
  98.2 10.8 %collective-permute-start.5 = (bf16[64,128]{1,0:T(8,128)(2,1)S(1)}, bf16[64,128]{1,0:T(8,128)(2,1)S(1)}, u32[]{:S(2)}, u32[]{:S(2)}) collective-permute-start(bf16[64,128]{1,0:T(8,128)(2,1)S(1)} %get-tuple-element.38.left_ref), channel_id=1, source_target_pairs={{0,0},{1,16},{2,2},{3,18},{4,4},{5,20},{6,6},{7,22},{8,8},{9,24},{... | collective-permute-start | bytes 49160 | tf_op jit(solution)/shard_map/ppermute | solution.py:379
  109.8 5.0 %copy-start = (bf16[256,32]{0,1:T(8,128)(2,1)S(1)}, bf16[256,32]{0,1:T(8,128)(2,1)}, u32[]{:S(2)}) copy-start(bf16[256,32]{0,1:T(8,128)(2,1)} %param.7) | copy-start | bytes 49156
  109.8 5.0 %copy-start.1 = (bf16[256,32]{0,1:T(8,128)(2,1)S(1)}, bf16[256,32]{0,1:T(8,128)(2,1)}, u32[]{:S(2)}) copy-start(bf16[256,32]{0,1:T(8,128)(2,1)} %param.8) | copy-start | bytes 49156
  109.8 12.1 %all-to-all-start.5 = ((bf16[8,128,128]{2,1,0:T(8,128)(2,1)}), bf16[8,128,128]{2,1,0:T(8,128)(2,1)S(1)}, u32[]{:S(2)}, u32[]{:S(2)}) async-start(bf16[8,128,128]{2,1,0:T(8,128)(2,1)} %broadcast_in_dim.7), calls=%async_computation.5 | async-start | bytes 524288 | tf_op jit(solution)/shard_map/all_to_all | solution.py:274
  121.9 4.2 %collective-permute-start.6 = (bf16[8,128,128]{2,1,0:T(8,128)(2,1)S(1)}, bf16[8,128,128]{2,1,0:T(8,128)(2,1)S(1)}, u32[]{:S(2)}, u32[]{:S(2)}) collective-permute-start(bf16[8,128,128]{2,1,0:T(8,128)(2,1)S(1)} %all-to-all-done.5.own_ref), channel_id=1, source_target_pairs={{0,32},{32,0},{1,33},{33,1},{2,34},{34,2},{3,35},{35,3},{4,36},{36... | collective-permute-start | bytes 786440 | tf_op jit(solution)/shard_map/ppermute | solution.py:283

commit v5 on v4

--- a/solution.py
+++ b/solution.py
@@ -140,9 +140,11 @@
 
 
 def pair_kernel(
-    blocks, cot_ref, w_turned_ref, bias_ref, pair_ref, keep_out, send_out,
-    gathered, spread, left_ref, outer, wout_sum, wout_rows,
+    blocks, cot_hbm, w_turned_ref, bias_ref, pair_ref, keep_out, send_out,
+    cot_ref, gathered, spread, left_ref, outer, wout_sum, wout_rows, arrived,
 ):
+    copy = pltpu.make_async_copy(cot_hbm, cot_ref, arrived)
+    copy.start()
     core = lax.axis_index("core")
     fill(blocks, left_ref, gathered, spread)
     left_ref[...] = (left_ref[...].astype(F32) * (1.0 / 64.0)).astype(BF16)
@@ -151,6 +153,7 @@
             piece = dot(left_ref[...], spread[h, d * 256 : d * 256 + 256, :], (1, 1)).astype(BF16)
             first = h * 128 + d * 32
             outer[:, first : first + 32, :] = piece.reshape(16, 32, 256)
+    copy.wait()
     for i in range(16):
         cot = cot_ref[i * 4 : i * 4 + 4].reshape(256, LANES)
         tile = outer[i]
@@ -339,15 +342,17 @@
     eight = struct((8, 64, LANES), BF16)
     pair, keep, send = pl.pallas_call(
         pair_kernel,
-        in_specs=[vm] * 4,
+        in_specs=[vm, hbm, vm, vm],
         out_shape=(struct((64, 64, LANES), BF16), eight, eight),
         scratch_shapes=[
+            vmem((64, 64, LANES), BF16),
             gathered,
             spread,
             left_rows,
             vmem((16, 1024, 256), BF16),
             vmem((1024, LANES), F32),
             vmem((1024, LANES), F32),
+            pltpu.SemaphoreType.DMA,
         ],
         compiler_params=params(24),
         cost_estimate=cost(4 << 30, 4 << 20),

time: 128 us -> 128 us (level)
  transfers between devices with their start and end apart: 11 -> 11, of which waited for: 8 -> 9; matrix products, arithmetic and copies ran while one was open for 0% -> 0% of each run, Pallas kernels for 8% -> 8%
where the time goes in v5:
time: 128 us; the launch traced here: 127 us
  starting transfers between devices  38.6 us (30%)
  waiting for transfers between devices  34.5 us (27%)
  blocking collectives  28.6 us (22%)
  Pallas kernels  22.3 us (17%)
  local copies, waits for them, and re-layouts  1.91 us (1%)
    all_to_all x2, blocking collectives, exchange(): return lax.all_to_all(value, axes, 0, 0, tiled=True)  28.6 us
    all_to_all x4, waiting for transfers between devices, exchange(): return lax.all_to_all(value, axes, 0, 0, tiled=True)  21.5 us
    all_to_all x4, starting transfers between devices, exchange(): return lax.all_to_all(value, axes, 0, 0, tiled=True)  20.7 us
    ppermute x4, starting transfers between devices, other_core(): return lax.ppermute(value, 'core', [(0, 1), (1, 0)])  11 us
    pallas_call x1, Pallas kernels, body(): pl.pallas_call(grads_kernel, in_specs=[vm, hbm, vm], out_shape=struct((16...  8.91 us
    ppermute x1, waiting for transfers between devices, body(): far_normed = lax.ppermute(normed, ('col', 'seq'), to_home)  8.69 us
    pallas_call x1, Pallas kernels, body(): pl.pallas_call(pair_kernel, in_specs=[vm, hbm, vm, vm], out_shape=(struct...  7.54 us
    ppermute x1, starting transfers between devices, body(): far_normed = lax.ppermute(far_normed, ('col', 'seq'), across)  4.96 us
  transfers between devices with their start and end apart: 11, of which 9 were waited for; matrix products, arithmetic and copies ran while one was open for 0% of the time, Pallas kernels for 8%

profile of v5, /device:TPU:1, one launch (start us, length us, event | category | flops | bytes accessed | tf_op | source)
XLA Modules:
  0.0 127.0 jit_solution(2714690357657228071)
XLA Ops:
  0.6 1.4 %project.1 = (bf16[8,128,128]{2,1,0:T(8,128)(2,1)S(1)}, bf16[256,256]{1,0:T(8,128)(2,1)S(1)}) custom-call(bf16[32,8,256]{2,1,0:T(8,128)(2,1)} %x_ref.3, bf16[32,256]{1,0:T(8,128)(2,1)} %bitcast.13, bf16[32,256]{1,0:T(8,128)(2,1)} %bitcast.15), custom_call_target="tpu_custom_call" | custom-call | tf_op jit(solution)/shard_map/project/pallas_call | solution.py:295
  2.1 15.9 %all_to_all.30.own_ref = bf16[8,128,128]{2,1,0:T(8,128)(2,1)S(1)} all-to-all(bf16[8,128,128]{2,1,0:T(8,128)(2,1)S(1)} %get-tuple-element.28), channel_id=1, replica_groups=mesh['z'=4,'core'=2,'col'=16,'seq'=2] {'z','seq'}, dimensions={0} | all-to-all | bytes 524288 | tf_op jit(solution)/shard_map/all_to_all | solution.py:277
  18.0 2.7 %collective-permute-start = (bf16[8,128,128]{2,1,0:T(8,128)(2,1)S(1)}, bf16[8,128,128]{2,1,0:T(8,128)(2,1)S(1)}, u32[]{:S(2)}, u32[]{:S(2)}) collective-permute-start(bf16[8,128,128]{2,1,0:T(8,128)(2,1)S(1)} %all_to_all.30.own_ref), channel_id=1, source_target_pairs={{0,32},{32,0},{1,33},{33,1},{2,34},{34,2},{3,35},{35,3},{4,36},{36... | collective-permute-start | bytes 786440 | tf_op jit(solution)/shard_map/ppermute | solution.py:286
  20.7 1.2 collective-permute-done.other_ref
  21.9 1.1 route.1
  23.0 0.0 copy-start.3
  23.0 6.9 %all-to-all-start.1 = ((bf16[16,256,128]{2,1,0:T(8,128)(2,1)}), bf16[16,256,128]{2,1,0:T(8,128)(2,1)S(1)}, u32[]{:S(2)}, u32[]{:S(2)}) async-start(bf16[16,256,128]{2,1,0:T(8,128)(2,1)} %route.1), calls=%async_computation.1 | async-start | bytes 2097152 | tf_op jit(solution)/shard_map/all_to_all | solution.py:277
  29.9 1.3 %collective-permute-start.1 = (bf16[256,256]{1,0:T(8,128)(2,1)S(1)}, bf16[256,256]{1,0:T(8,128)(2,1)S(1)}, u32[]{:S(2)}, u32[]{:S(2)}) collective-permute-start(bf16[256,256]{1,0:T(8,128)(2,1)S(1)} %get-tuple-element.29.normed_ref), channel_id=1, source_target_pairs={{1,0},{3,2},{5,4},{7,6},{9,8},{11,10},{13,12},{15,14},{16,17},{18,... | collective-permute-start | bytes 393224 | tf_op jit(solution)/shard_map/ppermute | solution.py:315
  31.2 0.0 copy-done.3
  31.2 0.1 copy.13
  31.3 0.1 multiply_convert_fusion.w_scaled_ref
  31.4 8.7 %collective-permute-done.1 = bf16[256,256]{1,0:T(8,128)(2,1)S(1)} collective-permute-done((bf16[256,256]{1,0:T(8,128)(2,1)S(1)}, bf16[256,256]{1,0:T(8,128)(2,1)S(1)}, u32[]{:S(2)}, u32[]{:S(2)}) %collective-permute-start.1) | collective-permute-done | bytes 131104 | tf_op jit(solution)/shard_map/ppermute | solution.py:315
  40.1 6.1 %all-to-all-done.1.blocks = bf16[16,256,128]{2,1,0:T(8,128)(2,1)S(1)} async-done(((bf16[16,256,128]{2,1,0:T(8,128)(2,1)}), bf16[16,256,128]{2,1,0:T(8,128)(2,1)S(1)}, u32[]{:S(2)}, u32[]{:S(2)}) %all-to-all-start.1) | async-done | bytes 1048608 | tf_op jit(solution)/shard_map/all_to_all | solution.py:277
  46.2 8.9 %grads.1 = bf16[16,192,128]{2,1,0:T(8,128)(2,1)} custom-call(bf16[16,256,128]{2,1,0:T(8,128)(2,1)S(1)} %all-to-all-done.1.blocks, bf16[64,64,128]{2,1,0:T(8,128)(2,1)} %cot_hbm.3, bf16[1024,128]{1,0:T(8,128)(2,1)S(1)} %multiply_convert_fusion.w_scaled_ref), custom_call_target="tpu_custom_call" | custom-call | flops 4294967296 | bytes 4194304 | tf_op jit(solution)/shard_map/grads/pallas_call | solution.py:320
  55.1 4.5 %all-to-all-start.2 = ((bf16[16,192,128]{2,1,0:T(8,128)(2,1)}), bf16[16,192,128]{2,1,0:T(8,128)(2,1)S(1)}, u32[]{:S(2)}, u32[]{:S(2)}) async-start(bf16[16,192,128]{2,1,0:T(8,128)(2,1)} %grads.1), calls=%async_computation.2 | async-start | bytes 1572864 | tf_op jit(solution)/shard_map/all_to_all | solution.py:277
  59.7 0.1 copy.14.w_turned_ref
  59.8 0.0 copy-start.2
  59.9 5.0 %collective-permute-start.2 = (bf16[256,256]{1,0:T(8,128)(2,1)S(1)}, bf16[256,256]{1,0:T(8,128)(2,1)S(1)}, u32[]{:S(2)}, u32[]{:S(2)}) collective-permute-start(bf16[256,256]{1,0:T(8,128)(2,1)S(1)} %collective-permute-done.1), channel_id=1, source_target_pairs={{0,16},{2,18},{4,20},{6,22},{8,24},{10,26},{12,28},{14,30},{17,1},... | collective-permute-start | bytes 393224 | tf_op jit(solution)/shard_map/ppermute | solution.py:340
  64.8 0.0 copy-done.2
  64.8 7.5 %pair_tile.1 = (bf16[64,64,128]{2,1,0:T(8,128)(2,1)}, bf16[8,64,128]{2,1,0:T(8,128)(2,1)S(1)}, bf16[8,64,128]{2,1,0:T(8,128)(2,1)S(1)}) custom-call(bf16[16,256,128]{2,1,0:T(8,128)(2,1)S(1)} %all-to-all-done.1.blocks, bf16[64,64,128]{2,1,0:T(8,128)(2,1)} %cot_hbm.3, bf16[128,1024]{1,0:T(8,128)(2,1)S(1)} %copy.14.w_turned_ref, f32[1,128]{1,0:T(1,128)S(1)} %bitcast.17), custom_call_target="tpu_custom_call" | custom-call | flops 4294967296 | bytes 4194304 | tf_op jit(solution)/shard_map/pair_tile/pallas_call | solution.py:343
  72.4 0.0 collective-permute-done.2.far_normed
  72.4 0.3 all-to-all-done.2.back_ref
  72.7 0.1 sort.1
  72.7 2.5 %collective-permute-start.3 = (bf16[8,128,128]{2,1,0:T(8,128)(2,1)S(1)}, bf16[8,128,128]{2,1,0:T(8,128)(2,1)S(1)}, u32[]{:S(2)}, u32[]{:S(2)}) collective-permute-start(bf16[8,128,128]{2,1,0:T(8,128)(2,1)S(1)} %get-tuple-element.40), channel_id=1, source_target_pairs={{0,32},{32,0},{1,33},{33,1},{2,34},{34,2},{3,35},{35,3},{4,36},{36... | collective-permute-start | bytes 786440 | tf_op jit(solution)/shard_map/ppermute | solution.py:286
  75.2 1.2 collective-permute-done.3
  76.4 0.1 add_convert_fusion
  76.4 12.7 %all_to_all.31 = bf16[8,128,128]{2,1,0:T(8,128)(2,1)S(1)} all-to-all(bf16[8,128,128]{2,1,0:T(8,128)(2,1)S(1)} %add_convert_fusion), channel_id=1, replica_groups=mesh['z'=4,'core'=2,'col'=16,'seq'=2] {'z','seq'}, dimensions={0} | all-to-all | bytes 524288 | tf_op jit(solution)/shard_map/all_to_all | solution.py:277
  89.2 0.2 weight_grads.1
  89.4 2.8 %collective-permute-start.4 = (bf16[64,128]{1,0:T(8,128)(2,1)S(1)}, bf16[64,128]{1,0:T(8,128)(2,1)S(1)}, u32[]{:S(2)}, u32[]{:S(2)}) collective-permute-start(bf16[64,128]{1,0:T(8,128)(2,1)S(1)} %get-tuple-element.43), channel_id=1, source_target_pairs={{0,32},{32,0},{1,33},{33,1},{2,34},{34,2},{3,35},{35,3},{4,36},{36... | collective-permute-start | bytes 49160 | tf_op jit(solution)/shard_map/ppermute | solution.py:286
  92.2 0.8 collective-permute-done.4
  93.1 0.9 broadcast_in_dim.6
  94.0 4.3 %all-to-all-start.4 = ((bf16[16,128,128]{2,1,0:T(8,128)(2,1)}), bf16[16,128,128]{2,1,0:T(8,128)(2,1)S(1)}, u32[]{:S(2)}, u32[]{:S(2)}) async-start(bf16[16,128,128]{2,1,0:T(8,128)(2,1)} %broadcast_in_dim.6), calls=%async_computation.4 | async-start | bytes 1048576 | tf_op jit(solution)/shard_map/all_to_all | solution.py:277
  98.2 0.7 collective-permute-start.5
  98.9 10.1 %all-to-all-done.4 = bf16[16,128,128]{2,1,0:T(8,128)(2,1)S(1)} async-done(((bf16[16,128,128]{2,1,0:T(8,128)(2,1)}), bf16[16,128,128]{2,1,0:T(8,128)(2,1)S(1)}, u32[]{:S(2)}, u32[]{:S(2)}) %all-to-all-start.4) | async-done | bytes 524320 | tf_op jit(solution)/shard_map/all_to_all | solution.py:277
  109.0 0.1 reduce_sum.25
  109.1 0.0 collective-permute-done.5.left_ref
  109.1 0.7 broadcast_in_dim.7
  109.8 0.0 copy-start
  109.8 0.0 copy-start.1
  109.8 5.0 %all-to-all-start.5 = ((bf16[8,128,128]{2,1,0:T(8,128)(2,1)}), bf16[8,128,128]{2,1,0:T(8,128)(2,1)S(1)}, u32[]{:S(2)}, u32[]{:S(2)}) async-start(bf16[8,128,128]{2,1,0:T(8,128)(2,1)} %broadcast_in_dim.7), calls=%async_computation.5 | async-start | bytes 524288 | tf_op jit(solution)/shard_map/all_to_all | solution.py:277
  114.8 0.0 copy-done
  114.8 0.0 copy-done.1
  114.8 2.1 %align.1 = f32[256,256]{1,0:T(8,128)} custom-call(bf16[32,8,256]{2,1,0:T(8,128)(2,1)} %x_ref.3, bf16[32,256]{1,0:T(8,128)(2,1)S(1)} %bitcast.14, bf16[32,256]{1,0:T(8,128)(2,1)S(1)} %bitcast.16, bf16[64,128]{1,0:T(8,128)(2,1)S(1)} %collective-permute-done.5.left_ref, bf16[64,128]{1,0:T(8,128)(2,1)S(1)} %get-tuple-element.51.right_ref), custom_call_target="tpu_custom_call" | custom-call | flops 16777216 | bytes 1048576 | tf_op jit(solution)/shard_map/align/pallas_call | solution.py:387
  116.9 5.0 %all-to-all-done.5.own_ref = bf16[8,128,128]{2,1,0:T(8,128)(2,1)S(1)} async-done(((bf16[8,128,128]{2,1,0:T(8,128)(2,1)}), bf16[8,128,128]{2,1,0:T(8,128)(2,1)S(1)}, u32[]{:S(2)}, u32[]{:S(2)}) %all-to-all-start.5) | async-done | bytes 262176 | tf_op jit(solution)/shard_map/all_to_all | solution.py:277
  121.9 3.0 %collective-permute-start.6 = (bf16[8,128,128]{2,1,0:T(8,128)(2,1)S(1)}, bf16[8,128,128]{2,1,0:T(8,128)(2,1)S(1)}, u32[]{:S(2)}, u32[]{:S(2)}) collective-permute-start(bf16[8,128,128]{2,1,0:T(8,128)(2,1)S(1)} %all-to-all-done.5.own_ref), channel_id=1, source_target_pairs={{0,32},{32,0},{1,33},{33,1},{2,34},{34,2},{3,35},{35,3},{4,36},{36... | collective-permute-start | bytes 786440 | tf_op jit(solution)/shard_map/ppermute | solution.py:286
  124.9 1.2 collective-permute-done.6.other_ref
  126.1 0.9 last.1
  (4 shorter events, 0.1 us)
Async XLA Ops:
  18.0 3.8 %collective-permute-start = (bf16[8,128,128]{2,1,0:T(8,128)(2,1)S(1)}, bf16[8,128,128]{2,1,0:T(8,128)(2,1)S(1)}, u32[]{:S(2)}, u32[]{:S(2)}) collective-permute-start(bf16[8,128,128]{2,1,0:T(8,128)(2,1)S(1)} %all_to_all.30.own_ref), channel_id=1, source_target_pairs={{0,32},{32,0},{1,33},{33,1},{2,34},{34,2},{3,35},{35,3},{4,36},{36... | collective-permute-start | bytes 786440 | tf_op jit(solution)/shard_map/ppermute | solution.py:286
  23.0 8.2 %copy-start.3 = (bf16[1024,128]{1,0:T(8,128)(2,1)S(1)}, bf16[1024,128]{1,0:T(8,128)(2,1)}, u32[]{:S(2)}) copy-start(bf16[1024,128]{1,0:T(8,128)(2,1)} %param.9) | copy-start | bytes 786436
  23.0 23.2 %all-to-all-start.1 = ((bf16[16,256,128]{2,1,0:T(8,128)(2,1)}), bf16[16,256,128]{2,1,0:T(8,128)(2,1)S(1)}, u32[]{:S(2)}, u32[]{:S(2)}) async-start(bf16[16,256,128]{2,1,0:T(8,128)(2,1)} %route.1), calls=%async_computation.1 | async-start | bytes 2097152 | tf_op jit(solution)/shard_map/all_to_all | solution.py:277
  29.9 10.2 %collective-permute-start.1 = (bf16[256,256]{1,0:T(8,128)(2,1)S(1)}, bf16[256,256]{1,0:T(8,128)(2,1)S(1)}, u32[]{:S(2)}, u32[]{:S(2)}) collective-permute-start(bf16[256,256]{1,0:T(8,128)(2,1)S(1)} %get-tuple-element.29.normed_ref), channel_id=1, source_target_pairs={{1,0},{3,2},{5,4},{7,6},{9,8},{11,10},{13,12},{15,14},{16,17},{18,... | collective-permute-start | bytes 393224 | tf_op jit(solution)/shard_map/ppermute | solution.py:315
  55.1 17.5 %all-to-all-start.2 = ((bf16[16,192,128]{2,1,0:T(8,128)(2,1)}), bf16[16,192,128]{2,1,0:T(8,128)(2,1)S(1)}, u32[]{:S(2)}, u32[]{:S(2)}) async-start(bf16[16,192,128]{2,1,0:T(8,128)(2,1)} %grads.1), calls=%async_computation.2 | async-start | bytes 1572864 | tf_op jit(solution)/shard_map/all_to_all | solution.py:277
  59.8 5.0 %copy-start.2 = (f32[128]{0:T(128)S(1)}, f32[128]{0:T(128)}, u32[]{:S(2)}) copy-start(f32[128]{0:T(128)} %param.10) | copy-start | bytes 1540
  59.9 12.5 %collective-permute-start.2 = (bf16[256,256]{1,0:T(8,128)(2,1)S(1)}, bf16[256,256]{1,0:T(8,128)(2,1)S(1)}, u32[]{:S(2)}, u32[]{:S(2)}) collective-permute-start(bf16[256,256]{1,0:T(8,128)(2,1)S(1)} %collective-permute-done.1), channel_id=1, source_target_pairs={{0,16},{2,18},{4,20},{6,22},{8,24},{10,26},{12,28},{14,30},{17,1},... | collective-permute-start | bytes 393224 | tf_op jit(solution)/shard_map/ppermute | solution.py:340
  72.7 3.7 %collective-permute-start.3 = (bf16[8,128,128]{2,1,0:T(8,128)(2,1)S(1)}, bf16[8,128,128]{2,1,0:T(8,128)(2,1)S(1)}, u32[]{:S(2)}, u32[]{:S(2)}) collective-permute-start(bf16[8,128,128]{2,1,0:T(8,128)(2,1)S(1)} %get-tuple-element.40), channel_id=1, source_target_pairs={{0,32},{32,0},{1,33},{33,1},{2,34},{34,2},{3,35},{35,3},{4,36},{36... | collective-permute-start | bytes 786440 | tf_op jit(solution)/shard_map/ppermute | solution.py:286
  89.4 3.6 %collective-permute-start.4 = (bf16[64,128]{1,0:T(8,128)(2,1)S(1)}, bf16[64,128]{1,0:T(8,128)(2,1)S(1)}, u32[]{:S(2)}, u32[]{:S(2)}) collective-permute-start(bf16[64,128]{1,0:T(8,128)(2,1)S(1)} %get-tuple-element.43), channel_id=1, source_target_pairs={{0,32},{32,0},{1,33},{33,1},{2,34},{34,2},{3,35},{35,3},{4,36},{36... | collective-permute-start | bytes 49160 | tf_op jit(solution)/shard_map/ppermute | solution.py:286
  94.0 15.0 %all-to-all-start.4 = ((bf16[16,128,128]{2,1,0:T(8,128)(2,1)}), bf16[16,128,128]{2,1,0:T(8,128)(2,1)S(1)}, u32[]{:S(2)}, u32[]{:S(2)}) async-start(bf16[16,128,128]{2,1,0:T(8,128)(2,1)} %broadcast_in_dim.6), calls=%async_computation.4 | async-start | bytes 1048576 | tf_op jit(solution)/shard_map/all_to_all | solution.py:277
  98.2 10.8 %collective-permute-start.5 = (bf16[64,128]{1,0:T(8,128)(2,1)S(1)}, bf16[64,128]{1,0:T(8,128)(2,1)S(1)}, u32[]{:S(2)}, u32[]{:S(2)}) collective-permute-start(bf16[64,128]{1,0:T(8,128)(2,1)S(1)} %get-tuple-element.38.left_ref), channel_id=1, source_target_pairs={{0,0},{1,16},{2,2},{3,18},{4,4},{5,20},{6,6},{7,22},{8,8},{9,24},{... | collective-permute-start | bytes 49160 | tf_op jit(solution)/shard_map/ppermute | solution.py:384
  109.8 5.0 %copy-start = (bf16[256,32]{0,1:T(8,128)(2,1)S(1)}, bf16[256,32]{0,1:T(8,128)(2,1)}, u32[]{:S(2)}) copy-start(bf16[256,32]{0,1:T(8,128)(2,1)} %param.7) | copy-start | bytes 49156
  109.8 5.0 %copy-start.1 = (bf16[256,32]{0,1:T(8,128)(2,1)S(1)}, bf16[256,32]{0,1:T(8,128)(2,1)}, u32[]{:S(2)}) copy-start(bf16[256,32]{0,1:T(8,128)(2,1)} %param.8) | copy-start | bytes 49156
  109.8 12.1 %all-to-all-start.5 = ((bf16[8,128,128]{2,1,0:T(8,128)(2,1)}), bf16[8,128,128]{2,1,0:T(8,128)(2,1)S(1)}, u32[]{:S(2)}, u32[]{:S(2)}) async-start(bf16[8,128,128]{2,1,0:T(8,128)(2,1)} %broadcast_in_dim.7), calls=%async_computation.5 | async-start | bytes 524288 | tf_op jit(solution)/shard_map/all_to_all | solution.py:277
  121.9 4.2 %collective-permute-start.6 = (bf16[8,128,128]{2,1,0:T(8,128)(2,1)S(1)}, bf16[8,128,128]{2,1,0:T(8,128)(2,1)S(1)}, u32[]{:S(2)}, u32[]{:S(2)}) collective-permute-start(bf16[8,128,128]{2,1,0:T(8,128)(2,1)S(1)} %all-to-all-done.5.own_ref), channel_id=1, source_target_pairs={{0,32},{32,0},{1,33},{33,1},{2,34},{34,2},{3,35},{35,3},{4,36},{36... | collective-permute-start | bytes 786440 | tf_op jit(solution)/shard_map/ppermute | solution.py:286
